TPU v7x, 512 devices: a whole 4x8x8 slice. The times are simulated.
512 devices in a mesh: leaf: 16 (over z, core), clusters: 32 (over x, y).
Axes of the slice: x: 4, y: 8, z: 8, core: 2. Of those that a mesh axis runs over, the one named last changes fastest.
Arguments:
- samples: float32 [262144, 256], P(('clusters', 'leaf')), may hold values from -6 to 6
- probes: float32 [262144, 256], P(('clusters', 'leaf')), may hold values from -6 to 6
- near_blocks: float32 [262144, 2, 512], P(('clusters', 'leaf')), may hold values from -0.15625 to 0.15625
- couplings: float32 [32, 15, 2, 128, 128], P('clusters'), may hold values from -0.375 to 0.375
- node_slot: int32 [32, 15], P('clusters'), may hold values from 0 to 14, each once within a row
Outputs:
- leaf_bases: float32 [262144, 128], P(('clusters', 'leaf'))
- transfer_bases: float32 [512, 4, 256, 128], P(('clusters', 'leaf'))
- top_samples: float32 [32, 128, 256], P('clusters')
- top_probes: float32 [32, 128, 256], P('clusters')
Inputs may be any that keep to these rules, and one draw needn't show every extreme that they name: Every row of node_slot names each of 0 to 14 exactly once.
All inputs are finite; a program needn't handle non-finite values.
Results may differ from a plain program's by a relative error of at most 0.00016.
Values sent between devices are 32-bit elements; how exact they have to be, the bound alone decides.
A program may use at most 64 MiB of HBM per device.

v0:
```python
import jax
import jax.numpy as jnp
from jax import lax
from jax.sharding import PartitionSpec as P

full_precision = lax.Precision.HIGHEST


def shifted(value, axis, by):
    peers = lax.axis_size(axis)
    return lax.ppermute(value, axis, [(i, (i + by) % peers) for i in range(peers)])


def shifted_2(value, axis, by):
    peers = lax.axis_size(axis)
    pairs = [(i, i + by) for i in range(peers) if 0 <= i + by < peers]
    return lax.ppermute(value, axis, pairs)


def from_partner(value, axis, stride):
    mask = 2**stride
    pairs = [(source, source ^ mask) for source in range(lax.axis_size(axis))]
    return lax.ppermute(value, axis, pairs)


def orthonormal(tall_block):
    gram_matrix = jnp.einsum("...rk,...rj->...kj", tall_block, tall_block, precision=full_precision)
    lower_factor = jnp.linalg.cholesky(gram_matrix)
    flipped = jax.scipy.linalg.solve_triangular(
        lower_factor, jnp.swapaxes(tall_block, -1, -2), lower=True
    )
    return jnp.swapaxes(flipped, -1, -2)


def project(node_basis, target):
    return jnp.einsum("...rk,...rs->...ks", node_basis, target, precision=full_precision)


def far_from_left(values, stride, subtree, member):
    if stride < subtree:
        inside = shifted(values, "leaf", stride)
        across = shifted_2(inside, "clusters", 1)
        return jnp.where(member < stride, across, inside)
    return shifted_2(values, "clusters", stride // subtree)


def far_from_right(values, stride, subtree, member):
    if stride < subtree:
        inside = shifted(values, "leaf", -stride)
        across = shifted_2(inside, "clusters", -1)
        return jnp.where(member >= subtree - stride, across, inside)
    return shifted_2(values, "clusters", -(stride // subtree))


def body(samples, probes, near_blocks, couplings, node_slot):
    columns = couplings.shape[-1]
    subtree = lax.axis_size("leaf")
    levels = subtree.bit_length() - 1
    member = lax.axis_index("leaf")
    diag_block = near_blocks[:, 0, :]
    upper_block = near_blocks[:, 1, :]
    handed = jnp.einsum("nm,ns->ms", upper_block, probes, precision=full_precision)
    lower_inner = shifted(handed, "leaf", 1)
    lower_outer = shifted_2(lower_inner, "clusters", 1)
    from_lower = jnp.where(member == 0, lower_outer, lower_inner)
    upper_inner = shifted(probes, "leaf", -1)
    upper_outer = shifted_2(upper_inner, "clusters", -1)
    from_upper = jnp.where(member == subtree - 1, upper_outer, upper_inner)
    diag_term = jnp.dot(
        diag_block, probes, precision=full_precision, preferred_element_type=jnp.float32
    )
    upper_term = jnp.dot(
        upper_block, from_upper, precision=full_precision, preferred_element_type=jnp.float32
    )
    far_samples = samples - diag_term - upper_term - from_lower
    leaf_basis = orthonormal(far_samples[:, :columns])
    sample_coef = project(leaf_basis, far_samples)
    probe_coef = project(leaf_basis, probes)
    slot_row = node_slot[0]
    coupling_table = couplings[0]
    ancestors = []
    for level_index in range(1, levels + 1):
        stride = 2**level_index
        from_left = far_from_left(probe_coef, stride, subtree, member)
        from_right = far_from_right(probe_coef, stride, subtree, member)
        parity = member >> level_index - 1 & 1
        main_far = jnp.where(parity == 0, from_left, from_right)
        other_far = jnp.where(parity == 0, from_right, from_left)
        node_index = subtree - (subtree >> level_index - 1) + (member >> level_index)
        slot_index = lax.dynamic_index_in_dim(slot_row, node_index, 0, keepdims=False)
        coupling_pair = lax.dynamic_index_in_dim(coupling_table, slot_index, 0, keepdims=False)
        coupling = lax.dynamic_index_in_dim(coupling_pair, parity, 0, keepdims=False)
        main_term = jnp.dot(
            coupling, main_far, precision=full_precision, preferred_element_type=jnp.float32
        )
        other_term = jnp.dot(
            coupling.T, other_far, precision=full_precision, preferred_element_type=jnp.float32
        )
        corrected = sample_coef - main_term - other_term
        sibling_samples, sibling_probes = from_partner(
            (corrected, probe_coef), "leaf", level_index - 1
        )
        lower_first = parity == 0
        stacked = jnp.where(
            lower_first,
            jnp.concatenate([corrected, sibling_samples], axis=0),
            jnp.concatenate([sibling_samples, corrected], axis=0),
        )
        stacked_probes = jnp.where(
            lower_first,
            jnp.concatenate([probe_coef, sibling_probes], axis=0),
            jnp.concatenate([sibling_probes, probe_coef], axis=0),
        )
        node_basis = orthonormal(stacked[:, :columns])
        ancestors.append(node_basis)
        sample_coef = project(node_basis, stacked)
        probe_coef = project(node_basis, stacked_probes)
    transfer_bases = jnp.stack(ancestors, axis=0)[None]
    return (leaf_basis, transfer_bases, sample_coef[None], probe_coef[None])


def solution(mesh):
    in_specs = (
        P(("clusters", "leaf"), None),
        P(("clusters", "leaf"), None),
        P(("clusters", "leaf"), None, None),
        P("clusters", None, None, None, None),
        P("clusters", None),
    )
    out_specs = (
        P(("clusters", "leaf"), None),
        P(("clusters", "leaf"), None, None, None),
        P("clusters", None, None),
        P("clusters", None, None),
    )
    return jax.shard_map(body, mesh=mesh, in_specs=in_specs, out_specs=out_specs, check_vma=False)
```

profile of v0, /device:TPU:6, one launch (start us, length us, event | category | flops | bytes accessed | tf_op | source)
XLA Modules:
  0.0 286.8 jit_solution(13108074470386454218)
XLA Ops:
  0.7 5.2 %fusion.123 = (f32[512,1,512]{2,1,0:T(1,128)S(1)}, f32[512,1,512]{2,1,0:T(1,128)}) fusion(f32[512,2,512]{2,1,0:T(2,128)} %param.10), kind=kLoop, calls=%fused_computation.173 | loop fusion | bytes 4194304 | tf_op jit(solution)/shard_map/slice | solution.py:61
  5.8 1.8 fusion.3
  7.7 8.5 %collective-permute-start = (f32[512,256]{1,0:T(8,128)S(1)}, f32[512,256]{1,0:T(8,128)}, u32[]{:S(2)}, u32[]{:S(2)}) collective-permute-start(f32[512,256]{1,0:T(8,128)S(1)} %copy-done.1), channel_id=1, source_target_pairs={{0,480},{32,0},{64,32},{96,64},{128,96},{160,128},{192,160},{224,1... | collective-permute-start | bytes 1572872 | tf_op jit(solution)/shard_map/ppermute | solution.py:11
  16.2 6.9 %collective-permute-done.2 = f32[512,256]{1,0:T(8,128)} collective-permute-done((f32[512,256]{1,0:T(8,128)S(1)}, f32[512,256]{1,0:T(8,128)}, u32[]{:S(2)}, u32[]{:S(2)}) %collective-permute-start.2) | collective-permute-done | bytes 524320 | tf_op jit(solution)/shard_map/ppermute | solution.py:11
  23.1 3.5 %collective-permute-start.3 = (f32[512,256]{1,0:T(8,128)}, f32[512,256]{1,0:T(8,128)}, u32[]{:S(2)}, u32[]{:S(2)}) collective-permute-start(f32[512,256]{1,0:T(8,128)} %collective-permute-done.2), channel_id=1, source_target_pairs={{0,1},{1,2},{2,3},{3,4},{4,5},{5,6},{6,7},{7,8},{8,9},{9,10},{10,1... | collective-permute-start | bytes 1572872 | tf_op jit(solution)/shard_map/ppermute | solution.py:17
  26.6 4.6 %collective-permute-start.1 = (f32[512,256]{1,0:T(8,128)}, f32[512,256]{1,0:T(8,128)}, u32[]{:S(2)}, u32[]{:S(2)}) collective-permute-start(f32[512,256]{1,0:T(8,128)} %collective-permute-done), channel_id=1, source_target_pairs={{1,0},{2,1},{3,2},{4,3},{5,4},{6,5},{7,6},{8,7},{9,8},{10,9},{11,1... | collective-permute-start | bytes 1572872 | tf_op jit(solution)/shard_map/ppermute | solution.py:17
  31.2 2.3 convolution_subtract_fusion
  33.6 3.0 %collective-permute-done.3 = f32[512,256]{1,0:T(8,128)} collective-permute-done((f32[512,256]{1,0:T(8,128)}, f32[512,256]{1,0:T(8,128)}, u32[]{:S(2)}, u32[]{:S(2)}) %collective-permute-start.3) | collective-permute-done | bytes 524320 | tf_op jit(solution)/shard_map/ppermute | solution.py:17
  36.6 1.5 collective-permute-done.1
  38.1 2.2 fusion.1
  41.0 11.7 %cholesky.89 = f32[128,128]{1,0:T(8,128)S(1)} custom-call(f32[128,128]{1,0:T(8,128)S(1)} %fusion.94), custom_call_target="Cholesky" | custom-call | tf_op jit(solution)/shard_map/jit(cholesky)/cholesky | solution.py:28
  54.1 9.8 %custom-call.9 = f32[1,128,128]{1,2,0:T(8,128)S(1)} custom-call(f32[1,128,128]{2,1,0:T(8,128)S(1)} %fusion.72), custom_call_target="InvertDiagBlocksLowerTriangular" | custom-call | tf_op jit(solution)/shard_map/jit(_solve_triangular)/triangular_solve | solution.py:29
  65.8 2.3 collective-permute-start.4
  68.1 7.2 %collective-permute-start.6 = (f32[128,256]{1,0:T(8,128)S(1)}, f32[128,256]{1,0:T(8,128)S(1)}, u32[]{:S(2)}, u32[]{:S(2)}) collective-permute-start(f32[128,256]{1,0:T(8,128)S(1)} %fusion.125), channel_id=1, source_target_pairs={{0,448},{32,480},{64,0},{96,32},{128,64},{160,96},{192,128},{224,1... | collective-permute-start | bytes 393224 | tf_op jit(solution)/shard_map/ppermute | solution.py:11
  77.9 2.2 collective-permute-start.5
  80.1 6.2 %collective-permute-start.7 = (f32[128,256]{1,0:T(8,128)S(1)}, f32[128,256]{1,0:T(8,128)S(1)}, u32[]{:S(2)}, u32[]{:S(2)}) collective-permute-start(f32[128,256]{1,0:T(8,128)S(1)} %collective-permute-done.6), channel_id=1, source_target_pairs={{1,0},{2,1},{3,2},{4,3},{5,4},{6,5},{7,6},{8,7},{9,8},{10,9},{11,1... | collective-permute-start | bytes 393224 | tf_op jit(solution)/shard_map/ppermute | solution.py:17
  87.3 1.5 collective-permute-done.7
  89.5 1.9 collective-permute-start.8
  91.4 2.6 collective-permute-start.9
  94.6 11.7 %cholesky.100 = f32[128,128]{1,0:T(8,128)S(1)} custom-call(f32[128,128]{1,0:T(8,128)S(1)} %fusion.90), custom_call_target="Cholesky" | custom-call | tf_op jit(solution)/shard_map/jit(cholesky)/cholesky | solution.py:28
  107.6 9.8 %custom-call.13 = f32[1,128,128]{1,2,0:T(8,128)S(1)} custom-call(f32[1,128,128]{2,1,0:T(8,128)S(1)} %fusion.73), custom_call_target="InvertDiagBlocksLowerTriangular" | custom-call | tf_op jit(solution)/shard_map/jit(_solve_triangular)/triangular_solve | solution.py:29
  118.1 2.0 collective-permute-start.10
  120.1 5.9 %collective-permute-start.12 = (f32[128,256]{1,0:T(8,128)S(1)}, f32[128,256]{1,0:T(8,128)S(1)}, u32[]{:S(2)}, u32[]{:S(2)}) collective-permute-start(f32[128,256]{1,0:T(8,128)S(1)} %fusion.5), channel_id=1, source_target_pairs={{0,384},{32,416},{64,448},{96,480},{128,0},{160,32},{192,64},{224,... | collective-permute-start | bytes 393224 | tf_op jit(solution)/shard_map/ppermute | solution.py:11
  128.0 2.3 collective-permute-done.10
  130.3 3.0 %collective-permute-start.11 = (f32[128,256]{1,0:T(8,128)S(1)}, f32[128,256]{1,0:T(8,128)S(1)}, u32[]{:S(2)}, u32[]{:S(2)}) collective-permute-start(f32[128,256]{1,0:T(8,128)S(1)} %collective-permute-done.10), channel_id=1, source_target_pairs={{0,1},{1,2},{2,3},{3,4},{4,5},{5,6},{6,7},{7,8},{8,9},{9,10},{10,1... | collective-permute-start | bytes 393224 | tf_op jit(solution)/shard_map/ppermute | solution.py:17
  133.3 5.5 %collective-permute-start.13 = (f32[128,256]{1,0:T(8,128)S(1)}, f32[128,256]{1,0:T(8,128)S(1)}, u32[]{:S(2)}, u32[]{:S(2)}) collective-permute-start(f32[128,256]{1,0:T(8,128)S(1)} %collective-permute-done.12), channel_id=1, source_target_pairs={{1,0},{2,1},{3,2},{4,3},{5,4},{6,5},{7,6},{8,7},{9,8},{10,9},{11,1... | collective-permute-start | bytes 393224 | tf_op jit(solution)/shard_map/ppermute | solution.py:17
  142.0 1.9 collective-permute-start.14
  143.9 4.2 %collective-permute-start.15 = (f32[128,256]{1,0:T(8,128)S(1)}, f32[128,256]{1,0:T(8,128)S(1)}, u32[]{:S(2)}, u32[]{:S(2)}) collective-permute-start(f32[128,256]{1,0:T(8,128)S(1)} %fusion.5), channel_id=1, source_target_pairs={{0,64},{32,96},{64,0},{96,32},{128,192},{160,224},{192,128},{224,1... | collective-permute-start | bytes 393224 | tf_op jit(solution)/shard_map/ppermute | solution.py:23
  148.1 1.9 collective-permute-done.14
  150.5 11.7 %cholesky.111 = f32[128,128]{1,0:T(8,128)S(1)} custom-call(f32[128,128]{1,0:T(8,128)S(1)} %fusion.86), custom_call_target="Cholesky" | custom-call | tf_op jit(solution)/shard_map/jit(cholesky)/cholesky | solution.py:28
  163.6 9.8 %custom-call.14 = f32[1,128,128]{1,2,0:T(8,128)S(1)} custom-call(f32[1,128,128]{2,1,0:T(8,128)S(1)} %fusion.74), custom_call_target="InvertDiagBlocksLowerTriangular" | custom-call | tf_op jit(solution)/shard_map/jit(_solve_triangular)/triangular_solve | solution.py:29
  174.0 5.9 %collective-permute-start.16 = (f32[128,256]{1,0:T(8,128)S(1)}, f32[128,256]{1,0:T(8,128)S(1)}, u32[]{:S(2)}, u32[]{:S(2)}) collective-permute-start(f32[128,256]{1,0:T(8,128)S(1)} %fusion.11), channel_id=1, source_target_pairs={{0,256},{32,288},{64,320},{96,352},{128,384},{160,416},{192,448},{... | collective-permute-start | bytes 393224 | tf_op jit(solution)/shard_map/ppermute | solution.py:11
  181.9 2.9 %collective-permute-done.16 = f32[128,256]{1,0:T(8,128)S(1)} collective-permute-done((f32[128,256]{1,0:T(8,128)S(1)}, f32[128,256]{1,0:T(8,128)S(1)}, u32[]{:S(2)}, u32[]{:S(2)}) %collective-permute-start.16) | collective-permute-done | bytes 131104 | tf_op jit(solution)/shard_map/ppermute | solution.py:11
  184.8 4.7 %collective-permute-start.17 = (f32[128,256]{1,0:T(8,128)S(1)}, f32[128,256]{1,0:T(8,128)S(1)}, u32[]{:S(2)}, u32[]{:S(2)}) collective-permute-start(f32[128,256]{1,0:T(8,128)S(1)} %collective-permute-done.16), channel_id=1, source_target_pairs={{0,1},{1,2},{2,3},{3,4},{4,5},{5,6},{6,7},{7,8},{8,9},{9,10},{10,1... | collective-permute-start | bytes 393224 | tf_op jit(solution)/shard_map/ppermute | solution.py:17
  189.4 3.4 %collective-permute-start.18 = (f32[128,256]{1,0:T(8,128)S(1)}, f32[128,256]{1,0:T(8,128)S(1)}, u32[]{:S(2)}, u32[]{:S(2)}) collective-permute-start(f32[128,256]{1,0:T(8,128)S(1)} %collective-permute-done.16), channel_id=1, source_target_pairs={{1,0},{2,1},{3,2},{4,3},{5,4},{6,5},{7,6},{8,7},{9,8},{10,9},{11,1... | collective-permute-start | bytes 393224 | tf_op jit(solution)/shard_map/ppermute | solution.py:17
  193.9 2.4 collective-permute-done.18
  196.9 5.6 %collective-permute-start.19 = (f32[128,256]{1,0:T(8,128)S(1)}, f32[128,256]{1,0:T(8,128)S(1)}, u32[]{:S(2)}, u32[]{:S(2)}) collective-permute-start(f32[128,256]{1,0:T(8,128)S(1)} %convolution_subtract_fusion.2), channel_id=1, source_target_pairs={{0,128},{32,160},{64,192},{96,224},{128,0},{160,32},{192,64},{224,... | collective-permute-start | bytes 393224 | tf_op jit(solution)/shard_map/ppermute | solution.py:23
  202.5 2.4 collective-permute-start.20
  204.9 3.1 %collective-permute-done.19 = f32[128,256]{1,0:T(8,128)S(1)} collective-permute-done((f32[128,256]{1,0:T(8,128)S(1)}, f32[128,256]{1,0:T(8,128)S(1)}, u32[]{:S(2)}, u32[]{:S(2)}) %collective-permute-start.19) | collective-permute-done | bytes 131104 | tf_op jit(solution)/shard_map/ppermute | solution.py:23
  208.6 11.7 %cholesky.122 = f32[128,128]{1,0:T(8,128)S(1)} custom-call(f32[128,128]{1,0:T(8,128)S(1)} %fusion.82), custom_call_target="Cholesky" | custom-call | tf_op jit(solution)/shard_map/jit(cholesky)/cholesky | solution.py:28
  221.6 9.8 %custom-call.15 = f32[1,128,128]{1,2,0:T(8,128)S(1)} custom-call(f32[1,128,128]{2,1,0:T(8,128)S(1)} %fusion.75), custom_call_target="InvertDiagBlocksLowerTriangular" | custom-call | tf_op jit(solution)/shard_map/jit(_solve_triangular)/triangular_solve | solution.py:29
  232.1 6.2 %collective-permute-start.22 = (f32[128,256]{1,0:T(8,128)S(1)}, f32[128,256]{1,0:T(8,128)S(1)}, u32[]{:S(2)}, u32[]{:S(2)}) collective-permute-start(f32[128,256]{1,0:T(8,128)S(1)} %fusion.17), channel_id=1, source_target_pairs={{1,0},{2,1},{3,2},{4,3},{5,4},{6,5},{7,6},{8,7},{9,8},{10,9},{11,1... | collective-permute-start | bytes 393224 | tf_op jit(solution)/shard_map/ppermute | solution.py:17
  238.2 1.9 collective-permute-start.21
  242.1 5.1 %collective-permute-done.21 = f32[128,256]{1,0:T(8,128)S(1)} collective-permute-done((f32[128,256]{1,0:T(8,128)S(1)}, f32[128,256]{1,0:T(8,128)S(1)}, u32[]{:S(2)}, u32[]{:S(2)}) %collective-permute-start.21) | collective-permute-done | bytes 131104 | tf_op jit(solution)/shard_map/ppermute | solution.py:17
  248.1 3.6 %collective-permute-start.23 = (f32[128,256]{1,0:T(8,128)S(1)}, f32[128,256]{1,0:T(8,128)S(1)}, u32[]{:S(2)}, u32[]{:S(2)}) collective-permute-start(f32[128,256]{1,0:T(8,128)S(1)} %fusion.2), channel_id=1, source_target_pairs={{0,256},{32,288},{64,320},{96,352},{128,384},{160,416},{192,448},{... | collective-permute-start | bytes 393224 | tf_op jit(solution)/shard_map/ppermute | solution.py:23
  252.5 6.3 %collective-permute-start.24 = (f32[128,256]{1,0:T(8,128)S(1)}, f32[128,256]{1,0:T(8,128)S(1)}, u32[]{:S(2)}, u32[]{:S(2)}) collective-permute-start(f32[128,256]{1,0:T(8,128)S(1)} %fusion.17), channel_id=1, source_target_pairs={{0,256},{32,288},{64,320},{96,352},{128,384},{160,416},{192,448},{... | collective-permute-start | bytes 393224 | tf_op jit(solution)/shard_map/ppermute | solution.py:23
  260.5 11.7 %cholesky.133 = f32[128,128]{1,0:T(8,128)S(1)} custom-call(f32[128,128]{1,0:T(8,128)S(1)} %fusion.78), custom_call_target="Cholesky" | custom-call | tf_op jit(solution)/shard_map/jit(cholesky)/cholesky | solution.py:28
  273.5 9.8 %custom-call.16 = f32[1,128,128]{1,2,0:T(8,128)S(1)} custom-call(f32[1,128,128]{2,1,0:T(8,128)S(1)} %fusion.76), custom_call_target="InvertDiagBlocksLowerTriangular" | custom-call | tf_op jit(solution)/shard_map/jit(_solve_triangular)/triangular_solve | solution.py:29
  (83 shorter events, 26.1 us)
Async XLA Ops:
  0.6 88.2 %copy-start = (f32[1,15,2,128,128]{4,3,2,1,0:T(8,128)S(1)}, f32[1,15,2,128,128]{4,3,2,1,0:T(8,128)}, u32[]{:S(2)}) copy-start(f32[1,15,2,128,128]{4,3,2,1,0:T(8,128)} %param.11) | copy-start | bytes 5898244
  0.6 5.2 %copy-start.1 = (f32[512,256]{1,0:T(8,128)S(1)}, f32[512,256]{1,0:T(8,128)}, u32[]{:S(2)}) copy-start(f32[512,256]{1,0:T(8,128)} %param.9) | copy-start | bytes 1572868
  7.6 15.5 %collective-permute-start.2 = (f32[512,256]{1,0:T(8,128)S(1)}, f32[512,256]{1,0:T(8,128)}, u32[]{:S(2)}, u32[]{:S(2)}) collective-permute-start(f32[512,256]{1,0:T(8,128)S(1)} %fusion.3), channel_id=1, source_target_pairs={{0,32},{32,64},{64,96},{96,128},{128,160},{160,192},{192,224},{224... | collective-permute-start | bytes 1572872 | tf_op jit(solution)/shard_map/ppermute | solution.py:11
  7.7 18.9 %collective-permute-start = (f32[512,256]{1,0:T(8,128)S(1)}, f32[512,256]{1,0:T(8,128)}, u32[]{:S(2)}, u32[]{:S(2)}) collective-permute-start(f32[512,256]{1,0:T(8,128)S(1)} %copy-done.1), channel_id=1, source_target_pairs={{0,480},{32,0},{64,32},{96,64},{128,96},{160,128},{192,160},{224,1... | collective-permute-start | bytes 1572872 | tf_op jit(solution)/shard_map/ppermute | solution.py:11
  23.1 13.5 %collective-permute-start.3 = (f32[512,256]{1,0:T(8,128)}, f32[512,256]{1,0:T(8,128)}, u32[]{:S(2)}, u32[]{:S(2)}) collective-permute-start(f32[512,256]{1,0:T(8,128)} %collective-permute-done.2), channel_id=1, source_target_pairs={{0,1},{1,2},{2,3},{3,4},{4,5},{5,6},{6,7},{7,8},{8,9},{9,10},{10,1... | collective-permute-start | bytes 1572872 | tf_op jit(solution)/shard_map/ppermute | solution.py:17
  26.6 11.5 %collective-permute-start.1 = (f32[512,256]{1,0:T(8,128)}, f32[512,256]{1,0:T(8,128)}, u32[]{:S(2)}, u32[]{:S(2)}) collective-permute-start(f32[512,256]{1,0:T(8,128)} %collective-permute-done), channel_id=1, source_target_pairs={{1,0},{2,1},{3,2},{4,3},{5,4},{6,5},{7,6},{8,7},{9,8},{10,9},{11,1... | collective-permute-start | bytes 1572872 | tf_op jit(solution)/shard_map/ppermute | solution.py:17
  40.3 35.0 %copy-start.2 = (s32[1,15]{1,0:T(1,128)S(1)}, s32[1,15]{1,0:T(1,128)}, u32[]{:S(2)}) copy-start(s32[1,15]{1,0:T(1,128)} %param.12) | copy-start | bytes 184
  65.8 12.1 %collective-permute-start.4 = (f32[128,256]{1,0:T(8,128)S(1)}, f32[128,256]{1,0:T(8,128)S(1)}, u32[]{:S(2)}, u32[]{:S(2)}) collective-permute-start(f32[128,256]{1,0:T(8,128)S(1)} %fusion.125), channel_id=1, source_target_pairs={{0,64},{32,96},{64,128},{96,160},{128,192},{160,224},{192,256},{22... | collective-permute-start | bytes 393224 | tf_op jit(solution)/shard_map/ppermute | solution.py:11
  68.1 12.0 %collective-permute-start.6 = (f32[128,256]{1,0:T(8,128)S(1)}, f32[128,256]{1,0:T(8,128)S(1)}, u32[]{:S(2)}, u32[]{:S(2)}) collective-permute-start(f32[128,256]{1,0:T(8,128)S(1)} %fusion.125), channel_id=1, source_target_pairs={{0,448},{32,480},{64,0},{96,32},{128,64},{160,96},{192,128},{224,1... | collective-permute-start | bytes 393224 | tf_op jit(solution)/shard_map/ppermute | solution.py:11
  77.9 9.4 %collective-permute-start.5 = (f32[128,256]{1,0:T(8,128)S(1)}, f32[128,256]{1,0:T(8,128)S(1)}, u32[]{:S(2)}, u32[]{:S(2)}) collective-permute-start(f32[128,256]{1,0:T(8,128)S(1)} %collective-permute-done.4), channel_id=1, source_target_pairs={{0,1},{1,2},{2,3},{3,4},{4,5},{5,6},{6,7},{7,8},{8,9},{9,10},{10,1... | collective-permute-start | bytes 393224 | tf_op jit(solution)/shard_map/ppermute | solution.py:17
  80.1 8.7 %collective-permute-start.7 = (f32[128,256]{1,0:T(8,128)S(1)}, f32[128,256]{1,0:T(8,128)S(1)}, u32[]{:S(2)}, u32[]{:S(2)}) collective-permute-start(f32[128,256]{1,0:T(8,128)S(1)} %collective-permute-done.6), channel_id=1, source_target_pairs={{1,0},{2,1},{3,2},{4,3},{5,4},{6,5},{7,6},{8,7},{9,8},{10,9},{11,1... | collective-permute-start | bytes 393224 | tf_op jit(solution)/shard_map/ppermute | solution.py:17
  89.5 4.6 %collective-permute-start.8 = (f32[128,256]{1,0:T(8,128)S(1)}, f32[128,256]{1,0:T(8,128)S(1)}, u32[]{:S(2)}, u32[]{:S(2)}) collective-permute-start(f32[128,256]{1,0:T(8,128)S(1)} %fusion.51), channel_id=1, source_target_pairs={{0,32},{32,0},{64,96},{96,64},{128,160},{160,128},{192,224},{224,1... | collective-permute-start | bytes 393224 | tf_op jit(solution)/shard_map/ppermute | solution.py:23
  91.4 26.4 %collective-permute-start.9 = (f32[128,256]{1,0:T(8,128)S(1)}, f32[128,256]{1,0:T(8,128)S(1)}, u32[]{:S(2)}, u32[]{:S(2)}) collective-permute-start(f32[128,256]{1,0:T(8,128)S(1)} %fusion.125), channel_id=1, source_target_pairs={{0,32},{32,0},{64,96},{96,64},{128,160},{160,128},{192,224},{224,1... | collective-permute-start | bytes 393224 | tf_op jit(solution)/shard_map/ppermute | solution.py:23
  118.1 12.2 %collective-permute-start.10 = (f32[128,256]{1,0:T(8,128)S(1)}, f32[128,256]{1,0:T(8,128)S(1)}, u32[]{:S(2)}, u32[]{:S(2)}) collective-permute-start(f32[128,256]{1,0:T(8,128)S(1)} %fusion.5), channel_id=1, source_target_pairs={{0,128},{32,160},{64,192},{96,224},{128,256},{160,288},{192,320},{... | collective-permute-start | bytes 393224 | tf_op jit(solution)/shard_map/ppermute | solution.py:11
  120.1 13.2 %collective-permute-start.12 = (f32[128,256]{1,0:T(8,128)S(1)}, f32[128,256]{1,0:T(8,128)S(1)}, u32[]{:S(2)}, u32[]{:S(2)}) collective-permute-start(f32[128,256]{1,0:T(8,128)S(1)} %fusion.5), channel_id=1, source_target_pairs={{0,384},{32,416},{64,448},{96,480},{128,0},{160,32},{192,64},{224,... | collective-permute-start | bytes 393224 | tf_op jit(solution)/shard_map/ppermute | solution.py:11
  130.3 9.9 %collective-permute-start.11 = (f32[128,256]{1,0:T(8,128)S(1)}, f32[128,256]{1,0:T(8,128)S(1)}, u32[]{:S(2)}, u32[]{:S(2)}) collective-permute-start(f32[128,256]{1,0:T(8,128)S(1)} %collective-permute-done.10), channel_id=1, source_target_pairs={{0,1},{1,2},{2,3},{3,4},{4,5},{5,6},{6,7},{7,8},{8,9},{9,10},{10,1... | collective-permute-start | bytes 393224 | tf_op jit(solution)/shard_map/ppermute | solution.py:17
  133.3 8.0 %collective-permute-start.13 = (f32[128,256]{1,0:T(8,128)S(1)}, f32[128,256]{1,0:T(8,128)S(1)}, u32[]{:S(2)}, u32[]{:S(2)}) collective-permute-start(f32[128,256]{1,0:T(8,128)S(1)} %collective-permute-done.12), channel_id=1, source_target_pairs={{1,0},{2,1},{3,2},{4,3},{5,4},{6,5},{7,6},{8,7},{9,8},{10,9},{11,1... | collective-permute-start | bytes 393224 | tf_op jit(solution)/shard_map/ppermute | solution.py:17
  142.0 8.0 %collective-permute-start.14 = (f32[128,256]{1,0:T(8,128)S(1)}, f32[128,256]{1,0:T(8,128)S(1)}, u32[]{:S(2)}, u32[]{:S(2)}) collective-permute-start(f32[128,256]{1,0:T(8,128)S(1)} %convolution_subtract_fusion.4), channel_id=1, source_target_pairs={{0,64},{32,96},{64,0},{96,32},{128,192},{160,224},{192,128},{224,1... | collective-permute-start | bytes 393224 | tf_op jit(solution)/shard_map/ppermute | solution.py:23
  143.9 29.8 %collective-permute-start.15 = (f32[128,256]{1,0:T(8,128)S(1)}, f32[128,256]{1,0:T(8,128)S(1)}, u32[]{:S(2)}, u32[]{:S(2)}) collective-permute-start(f32[128,256]{1,0:T(8,128)S(1)} %fusion.5), channel_id=1, source_target_pairs={{0,64},{32,96},{64,0},{96,32},{128,192},{160,224},{192,128},{224,1... | collective-permute-start | bytes 393224 | tf_op jit(solution)/shard_map/ppermute | solution.py:23
  174.0 10.8 %collective-permute-start.16 = (f32[128,256]{1,0:T(8,128)S(1)}, f32[128,256]{1,0:T(8,128)S(1)}, u32[]{:S(2)}, u32[]{:S(2)}) collective-permute-start(f32[128,256]{1,0:T(8,128)S(1)} %fusion.11), channel_id=1, source_target_pairs={{0,256},{32,288},{64,320},{96,352},{128,384},{160,416},{192,448},{... | collective-permute-start | bytes 393224 | tf_op jit(solution)/shard_map/ppermute | solution.py:11
  184.8 9.1 %collective-permute-start.17 = (f32[128,256]{1,0:T(8,128)S(1)}, f32[128,256]{1,0:T(8,128)S(1)}, u32[]{:S(2)}, u32[]{:S(2)}) collective-permute-start(f32[128,256]{1,0:T(8,128)S(1)} %collective-permute-done.16), channel_id=1, source_target_pairs={{0,1},{1,2},{2,3},{3,4},{4,5},{5,6},{6,7},{7,8},{8,9},{9,10},{10,1... | collective-permute-start | bytes 393224 | tf_op jit(solution)/shard_map/ppermute | solution.py:17
  189.4 6.9 %collective-permute-start.18 = (f32[128,256]{1,0:T(8,128)S(1)}, f32[128,256]{1,0:T(8,128)S(1)}, u32[]{:S(2)}, u32[]{:S(2)}) collective-permute-start(f32[128,256]{1,0:T(8,128)S(1)} %collective-permute-done.16), channel_id=1, source_target_pairs={{1,0},{2,1},{3,2},{4,3},{5,4},{6,5},{7,6},{8,7},{9,8},{10,9},{11,1... | collective-permute-start | bytes 393224 | tf_op jit(solution)/shard_map/ppermute | solution.py:17
  196.9 11.1 %collective-permute-start.19 = (f32[128,256]{1,0:T(8,128)S(1)}, f32[128,256]{1,0:T(8,128)S(1)}, u32[]{:S(2)}, u32[]{:S(2)}) collective-permute-start(f32[128,256]{1,0:T(8,128)S(1)} %convolution_subtract_fusion.2), channel_id=1, source_target_pairs={{0,128},{32,160},{64,192},{96,224},{128,0},{160,32},{192,64},{224,... | collective-permute-start | bytes 393224 | tf_op jit(solution)/shard_map/ppermute | solution.py:23
  202.5 29.2 %collective-permute-start.20 = (f32[128,256]{1,0:T(8,128)S(1)}, f32[128,256]{1,0:T(8,128)S(1)}, u32[]{:S(2)}, u32[]{:S(2)}) collective-permute-start(f32[128,256]{1,0:T(8,128)S(1)} %fusion.11), channel_id=1, source_target_pairs={{0,128},{32,160},{64,192},{96,224},{128,0},{160,32},{192,64},{224,... | collective-permute-start | bytes 393224 | tf_op jit(solution)/shard_map/ppermute | solution.py:23
  232.1 10.1 %collective-permute-start.22 = (f32[128,256]{1,0:T(8,128)S(1)}, f32[128,256]{1,0:T(8,128)S(1)}, u32[]{:S(2)}, u32[]{:S(2)}) collective-permute-start(f32[128,256]{1,0:T(8,128)S(1)} %fusion.17), channel_id=1, source_target_pairs={{1,0},{2,1},{3,2},{4,3},{5,4},{6,5},{7,6},{8,7},{9,8},{10,9},{11,1... | collective-permute-start | bytes 393224 | tf_op jit(solution)/shard_map/ppermute | solution.py:17
  238.2 9.0 %collective-permute-start.21 = (f32[128,256]{1,0:T(8,128)S(1)}, f32[128,256]{1,0:T(8,128)S(1)}, u32[]{:S(2)}, u32[]{:S(2)}) collective-permute-start(f32[128,256]{1,0:T(8,128)S(1)} %fusion.17), channel_id=1, source_target_pairs={{0,1},{1,2},{2,3},{3,4},{4,5},{5,6},{6,7},{7,8},{8,9},{9,10},{10,1... | collective-permute-start | bytes 393224 | tf_op jit(solution)/shard_map/ppermute | solution.py:17
  248.1 11.8 %collective-permute-start.23 = (f32[128,256]{1,0:T(8,128)S(1)}, f32[128,256]{1,0:T(8,128)S(1)}, u32[]{:S(2)}, u32[]{:S(2)}) collective-permute-start(f32[128,256]{1,0:T(8,128)S(1)} %fusion.2), channel_id=1, source_target_pairs={{0,256},{32,288},{64,320},{96,352},{128,384},{160,416},{192,448},{... | collective-permute-start | bytes 393224 | tf_op jit(solution)/shard_map/ppermute | solution.py:23
  252.5 33.1 %collective-permute-start.24 = (f32[128,256]{1,0:T(8,128)S(1)}, f32[128,256]{1,0:T(8,128)S(1)}, u32[]{:S(2)}, u32[]{:S(2)}) collective-permute-start(f32[128,256]{1,0:T(8,128)S(1)} %fusion.17), channel_id=1, source_target_pairs={{0,256},{32,288},{64,320},{96,352},{128,384},{160,416},{192,448},{... | collective-permute-start | bytes 393224 | tf_op jit(solution)/shard_map/ppermute | solution.py:23
where the time goes:
time: 291 us; the launch traced here: 287 us
  other arithmetic  114 us (39%)
  starting transfers between devices  102 us (35%)
  waiting for transfers between devices  35.2 us (12%)
  matrix products  18 us (6%)
  between operations  9.36 us (3%)
  local copies, waits for them, and re-layouts  8.06 us (3%)
    another operation x15, other arithmetic, orthonormal(): lower_factor = jnp.linalg.cholesky(gram_matrix)  61.9 us
    another operation x10, other arithmetic, orthonormal(): jax.scipy.linalg.solve_triangular(lower_factor, jnp.swapaxes(tall_block,...  52.3 us
    ppermute x10, starting transfers between devices, shifted_2(): return lax.ppermute(value, axis, pairs)  41.2 us
    ppermute x7, starting transfers between devices, shifted(): lax.ppermute(value, axis, [(i, (i + by) % peers) for i in range(peers)])  31.9 us
    ppermute x8, starting transfers between devices, from_partner(): return lax.ppermute(value, axis, pairs)  28.5 us
    ppermute x10, waiting for transfers between devices, shifted_2(): return lax.ppermute(value, axis, pairs)  17 us
    ppermute x7, waiting for transfers between devices, shifted(): lax.ppermute(value, axis, [(i, (i + by) % peers) for i in range(peers)])  12.1 us
    ppermute x8, waiting for transfers between devices, from_partner(): return lax.ppermute(value, axis, pairs)  6.08 us
  transfers between devices with their start and end apart: 25, of which 15 were waited for; matrix products, arithmetic and copies ran while one was open for 35% of the time, Pallas kernels for 0%

commit v1 on v0

v1 whole, which is shorter than its diff:
```python
import functools

import jax
import jax.numpy as jnp
from jax import lax
from jax.experimental import pallas as pl
from jax.experimental.pallas import tpu as pltpu
from jax.sharding import PartitionSpec as P

MESH = pl.DeviceIdType.MESH
f32 = jnp.float32
bf16 = jnp.bfloat16

K = 128
ROWS = 512
BLOCK = 8
REACH = 3


def halves(value):
    high = value.astype(bf16)
    return high, (value - high.astype(f32)).astype(bf16)


def product(a, b, contract=(1, 0)):
    dims = (((contract[0],), (contract[1],)), ((), ()))
    a_high, a_low = halves(a)
    b_high, b_low = halves(b)
    dot = functools.partial(lax.dot_general, dimension_numbers=dims, preferred_element_type=f32)
    return dot(a_high, b_high) + (dot(a_high, b_low) + dot(a_low, b_high))


def spread(block, column):
    return jnp.broadcast_to(block[:, column : column + 1], (block.shape[0], K))


def inverse_factor(gram, interludes):
    panels = K // BLOCK
    lane = lax.broadcasted_iota(jnp.int32, (BLOCK, K), 1)
    sub = lax.broadcasted_iota(jnp.int32, (BLOCK, K), 0)
    rounded = lambda v: v.astype(bf16).astype(f32)
    rows = [gram[BLOCK * g : BLOCK * (g + 1)] for g in range(panels)]
    pivot = [spread(rows[0], i) for i in range(BLOCK)]
    done = []
    for k in range(panels):
        if k in interludes:
            interludes[k]()
        first, after = BLOCK * k, BLOCK * (k + 1)
        near_end = min(panels, k + 1 + REACH)
        inside = (lane >= first) & (lane < after)
        panel = jnp.where(inside, (lane == first + sub).astype(f32), rows[k])
        below = coming = upcoming = far = None
        if k + 1 < panels:
            below = [spread(rows[k + 1], first + i) for i in range(BLOCK)]
            coming = [spread(rows[k + 1], after + i) for i in range(BLOCK)]
            upcoming = jnp.where(inside, 0.0, rows[k + 1])
        if near_end > k + 2:
            block = jnp.concatenate(rows[k + 2 : near_end], axis=0)
            far = [spread(block, first + i) for i in range(BLOCK)]
            wide = lax.broadcasted_iota(jnp.int32, block.shape, 1)
            far_rows = jnp.where((wide >= first) & (wide < after), 0.0, block)
        for i in range(BLOCK):
            scale = lax.rsqrt(pivot[i][i : i + 1, :])
            column = pivot[i] * scale
            row = panel[i : i + 1, :] * scale
            entry = [column[j : j + 1, :] for j in range(BLOCK)]
            for j in range(i + 1, BLOCK):
                pivot[j] = pivot[j] - column * entry[j]
            panel = jnp.where(sub == i, row, panel - jnp.where(sub > i, column, 0.0) * row)
            if below is not None:
                lower = below[i] * scale
                for j in range(i + 1, BLOCK):
                    below[j] = below[j] - lower * entry[j]
                for j in range(BLOCK):
                    coming[j] = coming[j] - lower * lower[j : j + 1, :]
                upcoming = upcoming - lower * row
            if far is not None:
                lowest = far[i] * scale
                for j in range(i + 1, BLOCK):
                    far[j] = far[j] - lowest * entry[j]
                far_rows = far_rows - lowest * row
        done.append(jnp.where(lane < after, panel, 0.0))
        pivot = coming
        if below is not None:
            rows[k + 1] = upcoming
        if far is not None:
            for g in range(k + 2, near_end):
                rows[g] = far_rows[BLOCK * (g - k - 2) : BLOCK * (g - k - 1)]
        if near_end < panels:
            high = rounded(panel)
            middle = rounded(panel - high)
            low = rounded(panel - high - middle)
            left = jnp.concatenate([high, high, middle, high, low, middle], axis=0).astype(bf16)
            right = jnp.concatenate([high, middle, high, low, high, middle], axis=0).astype(bf16)
            update = lax.dot_general(
                left, right, (((0,), (0,)), ((), ())), preferred_element_type=f32
            )
            for g in range(near_end, panels):
                rows[g] = jnp.where(inside, 0.0, rows[g]) - update[BLOCK * g : BLOCK * (g + 1)]
    return jnp.concatenate(done, axis=0)


def when(condition, run):
    if isinstance(condition, bool):
        if condition:
            run()
    else:
        pl.when(condition)(run)


def kernel(
    leaves, subtrees, slots, samples, probes, near, couplings,
    leaf_out, transfer_out, top_samples, top_probes,
    near_v, probes_v, samples_v, couplings_v,
    next_probes, handed, handed_in, far1, gram, inverse,
    second, stack1, wside1, z2, stack2, wside2,
    w1_out, w2_out, e1_out, e2_out,
    w1_in, w2_in, sib_in, q_leaf, q_top,
    local_sem, leaf_send, leaf_recv, send_sem, recv_sem, out_sem,
):
    levels = leaves.bit_length() - 1
    total = leaves * subtrees
    member = lax.axis_index("leaf")
    mine = lax.axis_index("clusters") * leaves + member

    def peer(offset):
        index = lax.rem(mine + offset + total, total)
        return {"leaf": lax.rem(index, leaves), "clusters": index // leaves}

    def send(source, target, sems, offset):
        copy = pltpu.make_async_remote_copy(
            src_ref=source, dst_ref=target, send_sem=sems[0], recv_sem=sems[1],
            device_id=peer(offset), device_id_type=MESH,
        )
        return copy

    loads = [
        pltpu.make_async_copy(near, near_v, local_sem.at[0]),
        pltpu.make_async_copy(probes, probes_v, local_sem.at[1]),
        pltpu.make_async_copy(samples, samples_v, local_sem.at[2]),
        pltpu.make_async_copy(couplings, couplings_v, local_sem.at[3]),
    ]
    for load in loads:
        load.start()

    barrier = pltpu.get_barrier_semaphore()
    distances = [1 << i for i in range(levels + 1)]
    for distance in distances:
        for offset in (distance, -distance):
            pl.semaphore_signal(barrier, inc=1, device_id=peer(offset), device_id_type=MESH)
    pl.semaphore_wait(barrier, 2 * len(distances))

    def leaf_probes(half):
        return send(
            probes.at[:, K * half : K * (half + 1)], next_probes.at[half],
            (leaf_send.at[half], leaf_recv.at[half]), -1,
        )

    def leaf_handed(half):
        return send(
            handed.at[half], handed_in.at[half],
            (leaf_send.at[2 + half], leaf_recv.at[2 + half]), 1,
        )

    leaf_probes(0).start()
    loads[1].wait()
    loads[0].wait()

    def near_block(which, column):
        return near_v[pl.ds(2 * column + which, ROWS, stride=8), :]

    def hand_over(half):
        own = probes_v[:, K * half : K * (half + 1)]
        for j in range(ROWS // K):
            handed[half, K * j : K * (j + 1), :] = product(near_block(1, j), own, (0, 0))

    def times(which, values):
        out = None
        for j in range(0, ROWS // K, 2):
            block = jnp.concatenate([near_block(which, j), near_block(which, j + 1)], axis=1)
            part = product(block, values[K * j : K * (j + 2)])
            out = part if out is None else out + part
        return out

    def far_half(half, first_wait):
        lanes = slice(K * half, K * (half + 1))
        part = samples_v[:, lanes] - times(0, probes_v[:, lanes])
        leaf_probes(half).wait_recv()
        last = mine == total - 1
        upper = jnp.where(last, 0.0, next_probes[half])
        part = part - times(1, upper)
        leaf_handed(half).wait_recv()
        return part - jnp.where(mine == 0, 0.0, handed_in[half])

    hand_over(0)
    leaf_handed(0).start()
    leaf_probes(1).start()
    loads[2].wait()
    far1[...] = far_half(0, None)
    own1 = probes_v[:, :K]
    gram[:, :K] = product(far1[...], far1[...], (0, 0))
    gram[:, K:] = product(far1[...], own1, (0, 0))
    hand_over(1)
    leaf_handed(1).start()
    loads[3].wait()

    def stage(s):
        distance = 1 << s if isinstance(s, int) else lax.shift_left(jnp.int32(1), s)
        parity = lax.rem(lax.shift_right_logical(member, jnp.int32(s)), 2)
        lower = parity == 0
        node = lax.shift_right_logical(mine, jnp.int32(s))
        nodes = lax.shift_right_logical(jnp.int32(total), jnp.int32(s))

        def exchange(kind, t):
            d = 1 << t if isinstance(t, int) else lax.shift_left(jnp.int32(1), t)
            par = lax.rem(lax.shift_right_logical(member, jnp.int32(t)), 2)
            sibling = d * (1 - 2 * par)
            source, target, offset = {
                0: (w1_out, w1_in.at[0], 2 * d), 1: (w1_out, w1_in.at[1], -2 * d), 2: (w1_out, sib_in.at[0], sibling),
                3: (w2_out, w2_in.at[0], 2 * d), 4: (w2_out, w2_in.at[1], -2 * d), 5: (w2_out, sib_in.at[1], sibling),
                6: (e1_out, sib_in.at[2], sibling), 7: (e2_out, sib_in.at[3], sibling),
            }[kind]
            return send(source.at[t], target.at[t], (send_sem.at[kind, t], recv_sem.at[kind, t]), offset)

        def coupling_sides(t):
            par = lax.rem(lax.shift_right_logical(member, jnp.int32(t)), 2)
            per = lax.shift_right_logical(jnp.int32(leaves), jnp.int32(t))
            index = leaves - per + lax.shift_right_logical(member, jnp.int32(t + 1))
            own = couplings_v[slots[index], par]
            turned = own.T
            even = par == 0
            return jnp.where(even, own, turned), jnp.where(even, turned, own)

        def correct(z, incoming, t):
            q = lax.shift_right_logical(mine, jnp.int32(t))
            count = lax.shift_right_logical(jnp.int32(total), jnp.int32(t))
            from_left, from_right = coupling_sides(t)
            left = jnp.where(q >= 2, incoming[0, t], 0.0)
            right = jnp.where(q < count - 2, incoming[1, t], 0.0)
            sides = jnp.concatenate([from_left, from_right], axis=1)
            return z - product(sides, jnp.concatenate([left, right], axis=0))

        def stacked(own, sibling, t):
            par = lax.rem(lax.shift_right_logical(member, jnp.int32(t)), 2)
            even = par == 0
            return jnp.concatenate([jnp.where(even, own, sibling), jnp.where(even, sibling, own)], axis=0)

        def leaf_second():
            far2 = far_half(1, None)
            second[:, :K] = product(far1[...], far2, (0, 0))
            second[:, K:] = product(far1[...], probes_v[:, K:], (0, 0))

        def level_second():
            t = s - 1
            exchange(3, t).wait_recv()
            exchange(4, t).wait_recv()
            e2_out[t] = correct(z2[...], w2_in, t)
            exchange(7, t).start()

        def level_second_end():
            t = s - 1
            exchange(5, t).wait_recv()
            exchange(7, t).wait_recv()
            second[:, :K] = product(stack1[...], stacked(e2_out[t], sib_in[3, t], t), (0, 0))
            second[:, K:] = product(stack1[...], stacked(w2_out[t], sib_in[1, t], t), (0, 0))

        def middle():
            when(s == 0, leaf_second)
            when(s > 0, level_second)

        inverse[...] = inverse_factor(gram[:, :K], {8: middle})
        x = inverse[...]

        def forward():
            w1_out[s] = product(x, gram[:, K:])
            for kind in range(3):
                exchange(kind, s).start()

        when(s < levels, forward)
        when(s > 0, level_second_end)

        z1 = product(x, gram[:, :K])
        zw2 = product(x, second[...])

        def leaf_basis():
            q_leaf[...] = product(far1[...], x, (1, 1))
            pltpu.make_async_copy(q_leaf, leaf_out, out_sem.at[levels]).start()

        def level_basis():
            t = s - 1
            q_top[t] = product(stack1[...], x, (1, 1))
            pltpu.make_async_copy(q_top.at[t], transfer_out.at[t], out_sem.at[t]).start()

        def go_on():
            z2[...] = zw2[:, :K]
            w2_out[s] = zw2[:, K:]
            when(s == 0, leaf_basis)
            when(s > 0, level_basis)
            exchange(0, s).wait_recv()
            exchange(1, s).wait_recv()
            e1_out[s] = correct(z1, w1_in, s)
            exchange(6, s).start()
            for kind in range(3, 6):
                exchange(kind, s).start()
            exchange(2, s).wait_recv()
            exchange(6, s).wait_recv()
            stack = stacked(e1_out[s], sib_in[2, s], s)
            stack1[...] = stack
            gram[:, :K] = product(stack, stack, (0, 0))
            gram[:, K:] = product(stack, stacked(w1_out[s], sib_in[0, s], s), (0, 0))

        def finish():
            top_samples[:, :K] = z1
            top_samples[:, K:] = zw2[:, :K]
            top_probes[:, :K] = product(x, gram[:, K:])
            top_probes[:, K:] = zw2[:, K:]
            level_basis()

        when(s < levels, go_on)
        when(s == levels, finish)
        return exchange

    if UNROLL:
        for s in range(levels + 1):
            exchange = stage(s)
    else:
        def step(s, carry):
            stage(s)
            return carry
        lax.fori_loop(0, levels + 1, step, 0)

    for half in range(2):
        leaf_probes(half).wait_send()
        leaf_handed(half).wait_send()
    for t in range(levels):
        sources = [w1_out] * 3 + [w2_out] * 3 + [e1_out, e2_out]
        for kind, source in enumerate(sources):
            send(source.at[t], source.at[t], (send_sem.at[kind, t], recv_sem.at[kind, t]), 1).wait_send()
        pltpu.make_async_copy(q_top.at[t], transfer_out.at[t], out_sem.at[t]).wait()
    pltpu.make_async_copy(q_leaf, leaf_out, out_sem.at[levels]).wait()


UNROLL = False


def solution(mesh):
    leaves, subtrees = mesh.shape["leaf"], mesh.shape["clusters"]
    levels = leaves.bit_length() - 1

    def body(samples, probes, near_blocks, couplings, node_slot):
        near = near_blocks.reshape(ROWS, 2, ROWS // K, K).transpose(0, 2, 1, 3).reshape(-1, K)
        anywhere = pl.BlockSpec(memory_space=pl.ANY)
        vmem = pl.BlockSpec(memory_space=pltpu.VMEM)
        leaf_basis, transfer, top_samples, top_probes = pl.pallas_call(
            functools.partial(kernel, leaves, subtrees),
            out_shape=(
                jax.ShapeDtypeStruct((ROWS, K), f32),
                jax.ShapeDtypeStruct((levels, 2 * K, K), f32),
                jax.ShapeDtypeStruct((K, 2 * K), f32),
                jax.ShapeDtypeStruct((K, 2 * K), f32),
            ),
            in_specs=[pl.BlockSpec(memory_space=pltpu.SMEM)] + [anywhere] * 4,
            out_specs=(anywhere, anywhere, vmem, vmem),
            scratch_shapes=[
                pltpu.VMEM((8 * ROWS, K), f32),
                pltpu.VMEM((ROWS, 2 * K), f32),
                pltpu.VMEM((ROWS, 2 * K), f32),
                pltpu.VMEM(couplings.shape[1:], f32),
                pltpu.VMEM((2, ROWS, K), f32),
                pltpu.VMEM((2, ROWS, K), f32),
                pltpu.VMEM((2, ROWS, K), f32),
                pltpu.VMEM((ROWS, K), f32),
                pltpu.VMEM((K, 2 * K), f32),
                pltpu.VMEM((K, K), f32),
                pltpu.VMEM((K, 2 * K), f32),
                pltpu.VMEM((2 * K, K), f32),
                pltpu.VMEM((2 * K, K), f32),
                pltpu.VMEM((K, K), f32),
                pltpu.VMEM((2 * K, K), f32),
                pltpu.VMEM((2 * K, K), f32),
                pltpu.VMEM((levels, K, K), f32),
                pltpu.VMEM((levels, K, K), f32),
                pltpu.VMEM((levels, K, K), f32),
                pltpu.VMEM((levels, K, K), f32),
                pltpu.VMEM((2, levels, K, K), f32),
                pltpu.VMEM((2, levels, K, K), f32),
                pltpu.VMEM((4, levels, K, K), f32),
                pltpu.VMEM((ROWS, K), f32),
                pltpu.VMEM((levels, 2 * K, K), f32),
                pltpu.SemaphoreType.DMA((4,)),
                pltpu.SemaphoreType.DMA((4,)),
                pltpu.SemaphoreType.DMA((4,)),
                pltpu.SemaphoreType.DMA((8, levels)),
                pltpu.SemaphoreType.DMA((8, levels)),
                pltpu.SemaphoreType.DMA((levels + 1,)),
            ],
            compiler_params=pltpu.CompilerParams(
                collective_id=0, has_side_effects=True, vmem_limit_bytes=60 * 2**20
            ),
            name="nested_bases",
        )(node_slot[0], samples, probes, near, couplings[0])
        return leaf_basis, transfer[None], top_samples[None], top_probes[None]

    in_specs = (
        P(("clusters", "leaf"), None),
        P(("clusters", "leaf"), None),
        P(("clusters", "leaf"), None, None),
        P("clusters", None, None, None, None),
        P("clusters", None),
    )
    out_specs = (
        P(("clusters", "leaf"), None),
        P(("clusters", "leaf"), None, None, None),
        P("clusters", None, None),
        P("clusters", None, None),
    )
    return jax.shard_map(body, mesh=mesh, in_specs=in_specs, out_specs=out_specs, check_vma=False)
```

time: 291 us -> 113 us (0.39)
  the two profiles are of different devices: /device:TPU:6 before, /device:TPU:64 now
where the time goes in v1:
time: 113 us
  Pallas kernels  106 us (94%)
  local copies, waits for them, and re-layouts  6.67 us (6%)
    pallas_call x1, Pallas kernels, body(): pl.pallas_call(functools.partial(kernel, leaves, subtrees), out_shape=(ja...  106 us
    unnamed x4, local copies, waits for them, and re-layouts  6.67 us

profile of v1, /device:TPU:64, one launch (start us, length us, event | category | flops | bytes accessed | tf_op | source)
XLA Modules:
  0.0 113.1 jit_solution(15331667449890913922)
XLA Ops:
  0.6 105.8 %nested_bases.1 = (f32[512,128]{1,0:T(8,128)}, f32[4,256,128]{2,1,0:T(8,128)}, f32[128,256]{1,0:T(8,128)}, f32[128,256]{1,0:T(8,128)}) custom-call(s32[15]{0:T(128)} %bitcast.15, f32[512,256]{1,0:T(8,128)} %samples.1, f32[512,256]{1,0:T(8,128)} %probes.1, f32[4096,128]{1,0:T(8,128)} %bitcast.10, f32[15,2,128,128]{3,2,1,0:T(8,128)} %bitcast.11), custom_call_target="tpu_custom_call" | custom-call | tf_op jit(solution)/shard_map/nested_bases/pallas_call | solution.py:354
  106.4 1.7 %copy.14 = f32[512,128]{1,0:T(8,128)} copy(f32[512,128]{1,0:T(8,128)} %get-tuple-element.16) | data formatting | bytes 524288
  108.1 1.9 %copy.15 = f32[1,4,256,128]{3,2,1,0:T(8,128)} copy(f32[1,4,256,128]{3,2,1,0:T(8,128)} %bitcast.12) | data formatting | bytes 1048576
  110.0 1.6 %copy.16 = f32[1,128,256]{2,1,0:T(8,128)} copy(f32[1,128,256]{2,1,0:T(8,128)} %bitcast.14) | data formatting | bytes 262144
  111.5 1.6 %copy.17 = f32[1,128,256]{2,1,0:T(8,128)} copy(f32[1,128,256]{2,1,0:T(8,128)} %bitcast.13) | data formatting | bytes 262144

commit v2 on v1

v2 whole, which is shorter than its diff:
```python
import functools

import jax
import jax.numpy as jnp
from jax import lax
from jax.experimental import pallas as pl
from jax.experimental.pallas import tpu as pltpu
from jax.sharding import PartitionSpec as P

MESH = pl.DeviceIdType.MESH
f32 = jnp.float32
bf16 = jnp.bfloat16

K = 128
ROWS = 512
BLOCK = 8
REACH = 3


def halves(value):
    high = value.astype(bf16)
    return high, (value - high.astype(f32)).astype(bf16)


def product(a, b, contract=(1, 0)):
    dims = (((contract[0],), (contract[1],)), ((), ()))
    a_high, a_low = halves(a)
    b_high, b_low = halves(b)
    dot = functools.partial(lax.dot_general, dimension_numbers=dims, preferred_element_type=f32)
    return dot(a_high, b_high) + (dot(a_high, b_low) + dot(a_low, b_high))


def spread(block, column):
    return jnp.broadcast_to(block[:, column : column + 1], (block.shape[0], K))


def inverse_factor(gram, interludes):
    panels = K // BLOCK
    lane = lax.broadcasted_iota(jnp.int32, (BLOCK, K), 1)
    sub = lax.broadcasted_iota(jnp.int32, (BLOCK, K), 0)
    rounded = lambda v: v.astype(bf16).astype(f32)
    rows = [gram[BLOCK * g : BLOCK * (g + 1)] for g in range(panels)]
    pivot = [spread(rows[0], i) for i in range(BLOCK)]
    done = []
    for k in range(panels):
        if k in interludes:
            interludes[k]()
        first, after = BLOCK * k, BLOCK * (k + 1)
        near_end = min(panels, k + 1 + REACH)
        inside = (lane >= first) & (lane < after)
        panel = jnp.where(inside, (lane == first + sub).astype(f32), rows[k])
        below = coming = upcoming = far = None
        if k + 1 < panels:
            below = [spread(rows[k + 1], first + i) for i in range(BLOCK)]
            coming = [spread(rows[k + 1], after + i) for i in range(BLOCK)]
            upcoming = jnp.where(inside, 0.0, rows[k + 1])
        if near_end > k + 2:
            block = jnp.concatenate(rows[k + 2 : near_end], axis=0)
            far = [spread(block, first + i) for i in range(BLOCK)]
            wide = lax.broadcasted_iota(jnp.int32, block.shape, 1)
            far_rows = jnp.where((wide >= first) & (wide < after), 0.0, block)
        for i in range(BLOCK):
            scale = lax.rsqrt(pivot[i][i : i + 1, :])
            column = pivot[i] * scale
            row = panel[i : i + 1, :] * scale
            entry = [column[j : j + 1, :] for j in range(BLOCK)]
            for j in range(i + 1, BLOCK):
                pivot[j] = pivot[j] - column * entry[j]
            panel = jnp.where(sub == i, row, panel - jnp.where(sub > i, column, 0.0) * row)
            if below is not None:
                lower = below[i] * scale
                for j in range(i + 1, BLOCK):
                    below[j] = below[j] - lower * entry[j]
                for j in range(BLOCK):
                    coming[j] = coming[j] - lower * lower[j : j + 1, :]
                upcoming = upcoming - lower * row
            if far is not None:
                lowest = far[i] * scale
                for j in range(i + 1, BLOCK):
                    far[j] = far[j] - lowest * entry[j]
                far_rows = far_rows - lowest * row
        done.append(jnp.where(lane < after, panel, 0.0))
        pivot = coming
        if below is not None:
            rows[k + 1] = upcoming
        if far is not None:
            for g in range(k + 2, near_end):
                rows[g] = far_rows[BLOCK * (g - k - 2) : BLOCK * (g - k - 1)]
        if near_end < panels:
            high = rounded(panel)
            middle = rounded(panel - high)
            low = rounded(panel - high - middle)
            left = jnp.concatenate([high, high, middle, high, low, middle], axis=0).astype(bf16)
            right = jnp.concatenate([high, middle, high, low, high, middle], axis=0).astype(bf16)
            update = lax.dot_general(
                left, right, (((0,), (0,)), ((), ())), preferred_element_type=f32
            )
            for g in range(near_end, panels):
                rows[g] = jnp.where(inside, 0.0, rows[g]) - update[BLOCK * g : BLOCK * (g + 1)]
    return jnp.concatenate(done, axis=0)


GROUPS = 3


def kernel(
    leaves, subtrees, slots, samples, probes, near, couplings,
    leaf_out, transfer_out, top_samples, top_probes,
    near_v, probes_v, samples_v, couplings_v, next_probes, handed, handed_in, far1,
    gram, inverse, inner, sent, far_in, corrected, passed, gathered, q_leaf, q_top,
    local_sem, leaf_send, leaf_recv, far_send, far_recv, pass_send, pass_recv,
    join_send, join_recv, last_send, last_recv, out_sem,
):
    levels = leaves.bit_length() - 1
    total = leaves * subtrees
    member = lax.axis_index("leaf")
    cluster = lax.axis_index("clusters")
    mine = cluster * leaves + member

    def along(offset):
        index = lax.rem(mine + offset + total, total)
        return {"leaf": lax.rem(index, leaves), "clusters": index // leaves}

    def across(mask):
        return {"leaf": jnp.bitwise_xor(member, mask), "clusters": cluster}

    def send(source, target, sems, device):
        return pltpu.make_async_remote_copy(
            src_ref=source, dst_ref=target, send_sem=sems[0], recv_sem=sems[1],
            device_id=device, device_id_type=MESH,
        )

    def bit(i):
        return lax.rem(lax.shift_right_logical(member, jnp.int32(i)), 2)

    def width(t):
        return K >> t

    def begin(t):
        start = jnp.int32(0)
        for i in range(t):
            start = start + bit(i) * (K >> (i + 1))
        return pl.multiple_of(start, BLOCK)

    barrier = pltpu.get_barrier_semaphore()
    peers = [along(side << i) for i in range(levels + 1) for side in (1, -1)]
    peers += [across(mask) for mask in range(1, leaves)]
    for peer in peers:
        pl.semaphore_signal(barrier, inc=1, device_id=peer, device_id_type=MESH)

    loads = [
        pltpu.make_async_copy(near, near_v, local_sem.at[0]),
        pltpu.make_async_copy(probes, probes_v, local_sem.at[1]),
        pltpu.make_async_copy(samples, samples_v, local_sem.at[2]),
        pltpu.make_async_copy(couplings, couplings_v, local_sem.at[3]),
    ]
    for load in loads:
        load.start()

    def leaf_probes(half):
        return send(
            probes.at[:, K * half : K * (half + 1)], next_probes.at[half],
            (leaf_send.at[half], leaf_recv.at[half]), along(-1),
        )

    def leaf_handed(half):
        return send(
            handed.at[half], handed_in.at[half],
            (leaf_send.at[2 + half], leaf_recv.at[2 + half]), along(1),
        )

    def near_block(which, column):
        return near_v[pl.ds(2 * column + which, ROWS, stride=8), :]

    def times(which, values):
        out = None
        for j in range(0, ROWS // K, 2):
            block = jnp.concatenate([near_block(which, j), near_block(which, j + 1)], axis=1)
            part = product(block, values[K * j : K * (j + 2)])
            out = part if out is None else out + part
        return out

    loads[0].wait()
    loads[1].wait()
    for j in range(ROWS // K):
        block = product(near_block(1, j), probes_v[...], (0, 0))
        handed[0, K * j : K * (j + 1), :] = block[:, :K]
        handed[1, K * j : K * (j + 1), :] = block[:, K:]
    loads[2].wait()
    samples_v[...] = samples_v[...] - times(0, probes_v[...])

    pl.semaphore_wait(barrier, len(peers))
    for half in range(2):
        leaf_handed(half).start()
        leaf_probes(half).start()
    def far_half(half):
        leaf_probes(half).wait_recv()
        upper = jnp.where(mine == total - 1, 0.0, next_probes[half])
        part = samples_v[:, K * half : K * (half + 1)] - times(1, upper)
        leaf_handed(half).wait_recv()
        return part - jnp.where(mine == 0, 0.0, handed_in[half])

    far1[...] = far_half(0)
    gram[...] = product(far1[...], far1[...], (0, 0))

    def far_copy(t, group, side):
        n = width(t)
        return send(
            sent.at[t, group, pl.ds(0, n)], far_in.at[side, t, group, pl.ds(0, n)],
            (far_send.at[side, t, group], far_recv.at[side, t, group]), along((2 << t) * (1 - 2 * side)),
        )

    def pass_copy(t):
        n = width(t) // 2
        away = pl.multiple_of((1 - bit(t)) * n, BLOCK)
        return send(
            sent.at[t, :, pl.ds(away, n)], passed.at[t, :, pl.ds(0, n)],
            (pass_send.at[t], pass_recv.at[t]), across(1 << t),
        )

    def join_copy(t, mask):
        part = corrected.at[t, bit(t), pl.ds(begin(t), width(t))]
        return send(part, part, (join_send.at[t, mask], join_recv.at[t, mask]), across(mask))

    def last_copy(mask):
        part = gathered.at[:, pl.ds(begin(levels), width(levels))]
        return send(part, part, (last_send.at[mask], last_recv.at[mask]), across(mask))

    def far_order(count):
        return sorted(range(1, count), key=lambda mask: -mask)

    def leaf_second():
        loads[3].wait()
        far2 = far_half(1)
        tall = jnp.concatenate([far2, probes_v[:, K:], probes_v[:, :K]], axis=1)
        block = product(tall, far1[...], (0, 0))
        for group in range(GROUPS):
            inner[group] = block[K * group : K * (group + 1)]

    def leaf_basis():
        q_leaf[...] = product(far1[...], inverse[...], (1, 1))
        pltpu.make_async_copy(q_leaf, leaf_out, out_sem.at[levels]).start()

    def level_basis(t):
        x = inverse[...]
        for child in range(2):
            q_top[t, K * child : K * (child + 1), :] = product(corrected[t, child], x, (0, 1))
        pltpu.make_async_copy(q_top.at[t], transfer_out.at[t], out_sem.at[t]).start()

    def merge(t):
        n = width(t)
        x = inverse[...]
        sent[t, 2, :n] = product(inner[2, :n], x, (1, 1))
        far_copy(t, 2, 0).start()
        far_copy(t, 2, 1).start()
        both = product(jnp.concatenate([inner[1, :n], inner[0, :n]], axis=0), x, (1, 1))
        sent[t, 1, :n] = both[:n]
        far_copy(t, 1, 0).start()
        far_copy(t, 1, 1).start()
        own = product(gram[pl.ds(begin(t), n)], x, (1, 1))
        per = leaves >> t
        index = leaves - per + lax.shift_right_logical(member, jnp.int32(t + 1))
        coupling = couplings_v[slots[index], bit(t)]
        turned = coupling.T
        even = bit(t) == 0
        sides = jnp.concatenate([jnp.where(even, coupling, turned), jnp.where(even, turned, coupling)], axis=1)
        node = lax.shift_right_logical(mine, jnp.int32(t))
        has_left, has_right = node >= 2, node < (total >> t) - 2
        if t == 0:
            leaf_basis()
        else:
            level_basis(t - 1)

        def correct(z, group):
            left = jnp.where(has_left, far_in[0, t, group, :n], 0.0)
            right = jnp.where(has_right, far_in[1, t, group, :n], 0.0)
            return z - product(jnp.concatenate([left, right], axis=1), sides, (1, 1))

        far_copy(t, 2, 0).wait_recv()
        far_copy(t, 2, 1).wait_recv()
        corrected[t, bit(t), pl.ds(begin(t), n)] = correct(own, 2)
        for mask in far_order(2 << t):
            join_copy(t, mask).start()
        far_copy(t, 1, 0).wait_recv()
        far_copy(t, 1, 1).wait_recv()
        sent[t, 0, :n] = correct(both[n:], 1)
        pass_copy(t).start()

        for mask in far_order(2 << t):
            join_copy(t, mask).wait_recv()
        wide = jnp.concatenate([corrected[t, 0], corrected[t, 1]], axis=1)
        gram[...] = product(wide, wide, (1, 1))
        pass_copy(t).wait_recv()
        h = n // 2
        keep = pl.multiple_of(bit(t) * h, BLOCK)
        kept = jnp.concatenate([sent[t, group, pl.ds(keep, h)] for group in range(GROUPS)], axis=0)
        came = jnp.concatenate([passed[t, group, :h] for group in range(GROUPS)], axis=0)
        pair = jnp.concatenate([jnp.where(even, kept, came), jnp.where(even, came, kept)], axis=1)
        block = product(pair, wide, (1, 1))
        if t + 1 < levels:
            for group in range(GROUPS):
                inner[group, :h] = block[h * group : h * (group + 1)]
        else:
            for group in range(GROUPS):
                gathered[group, pl.ds(begin(levels), h)] = block[h * group : h * (group + 1)]
            for mask in far_order(leaves):
                last_copy(mask).start()

    def finish():
        x = inverse[...]
        level_basis(levels - 1)
        top_samples[:, :K] = product(x, gram[...], (1, 1))
        for mask in far_order(leaves):
            last_copy(mask).wait_recv()
        block = product(x, jnp.concatenate([gathered[group] for group in range(GROUPS)], axis=0), (1, 1))
        top_samples[:, K:] = block[:, :K]
        top_probes[:, K:] = block[:, K : 2 * K]
        top_probes[:, :K] = block[:, 2 * K :]

    def step(s, carry):
        inverse[...] = inverse_factor(gram[...], {8: lambda: pl.when(s == 0)(leaf_second)})
        for t in range(levels):
            pl.when(s == t)(functools.partial(merge, t))
        pl.when(s == levels)(finish)
        return carry

    lax.fori_loop(0, levels + 1, step, 0)

    for half in range(2):
        leaf_probes(half).wait_send()
        leaf_handed(half).wait_send()
    for t in range(levels):
        for group in (2, 1):
            for side in range(2):
                far_copy(t, group, side).wait_send()
        pass_copy(t).wait_send()
        for mask in far_order(2 << t):
            join_copy(t, mask).wait_send()
        pltpu.make_async_copy(q_top.at[t], transfer_out.at[t], out_sem.at[t]).wait()
    for mask in far_order(leaves):
        last_copy(mask).wait_send()
    pltpu.make_async_copy(q_leaf, leaf_out, out_sem.at[levels]).wait()


def hand_out(*refs):
    count = len(refs) // 2
    for i in range(count):
        refs[count + i][...] = refs[i][...]


def solution(mesh):
    leaves, subtrees = mesh.shape["leaf"], mesh.shape["clusters"]
    levels = leaves.bit_length() - 1

    def body(samples, probes, near_blocks, couplings, node_slot):
        near = near_blocks.reshape(ROWS, 2, ROWS // K, K).transpose(0, 2, 1, 3).reshape(-1, K)
        anywhere = pl.BlockSpec(memory_space=pl.ANY)
        vmem = pl.BlockSpec(memory_space=pltpu.VMEM)
        shapes = (
            jax.ShapeDtypeStruct((ROWS, K), f32),
            jax.ShapeDtypeStruct((levels, 2 * K, K), f32),
            jax.ShapeDtypeStruct((K, 2 * K), f32),
            jax.ShapeDtypeStruct((K, 2 * K), f32),
        )
        dma = pltpu.SemaphoreType.DMA
        results = pl.pallas_call(
            functools.partial(kernel, leaves, subtrees),
            out_shape=shapes,
            in_specs=[pl.BlockSpec(memory_space=pltpu.SMEM)] + [anywhere] * 4,
            out_specs=(anywhere, anywhere, vmem, vmem),
            scratch_shapes=[
                pltpu.VMEM((8 * ROWS, K), f32),
                pltpu.VMEM((ROWS, 2 * K), f32),
                pltpu.VMEM((ROWS, 2 * K), f32),
                pltpu.VMEM(couplings.shape[1:], f32),
                pltpu.VMEM((2, ROWS, K), f32),
                pltpu.VMEM((2, ROWS, K), f32),
                pltpu.VMEM((2, ROWS, K), f32),
                pltpu.VMEM((ROWS, K), f32),
                pltpu.VMEM((K, K), f32),
                pltpu.VMEM((K, K), f32),
                pltpu.VMEM((GROUPS, K, K), f32),
                pltpu.VMEM((levels, GROUPS, K, K), f32),
                pltpu.VMEM((2, levels, GROUPS, K, K), f32),
                pltpu.VMEM((levels, 2, K, K), f32),
                pltpu.VMEM((levels, GROUPS, K // 2, K), f32),
                pltpu.VMEM((GROUPS, K, K), f32),
                pltpu.VMEM((ROWS, K), f32),
                pltpu.VMEM((levels, 2 * K, K), f32),
                dma((4,)), dma((4,)), dma((4,)),
                dma((2, levels, GROUPS)), dma((2, levels, GROUPS)),
                dma((levels,)), dma((levels,)),
                dma((levels, leaves)), dma((levels, leaves)),
                dma((leaves,)), dma((leaves,)),
                dma((levels + 1,)),
            ],
            compiler_params=pltpu.CompilerParams(
                collective_id=0, has_side_effects=True, vmem_limit_bytes=60 * 2**20
            ),
            name="nested_bases",
        )(node_slot[0], samples, probes, near, couplings[0])
        leaf_basis, transfer, top_samples, top_probes = pl.pallas_call(
            hand_out,
            out_shape=shapes,
            in_specs=[vmem] * 4,
            out_specs=(vmem,) * 4,
            name="hand_out",
        )(*results)
        return leaf_basis, transfer[None], top_samples[None], top_probes[None]

    in_specs = (
        P(("clusters", "leaf"), None),
        P(("clusters", "leaf"), None),
        P(("clusters", "leaf"), None, None),
        P("clusters", None, None, None, None),
        P("clusters", None),
    )
    out_specs = (
        P(("clusters", "leaf"), None),
        P(("clusters", "leaf"), None, None, None),
        P("clusters", None, None),
        P("clusters", None, None),
    )
    return jax.shard_map(body, mesh=mesh, in_specs=in_specs, out_specs=out_specs, check_vma=False)
```

time: 113 us -> 90.5 us (0.80)
  the two profiles are of different devices: /device:TPU:64 before, /device:TPU:1 now
where the time goes in v2:
time: 90.5 us; the launch traced here: 90.4 us
  Pallas kernels  89.7 us (99%)
    pallas_call x1, Pallas kernels, body(): pl.pallas_call(functools.partial(kernel, leaves, subtrees), out_shape=sha...  87.6 us
    pallas_call x1, Pallas kernels, body(): pl.pallas_call(hand_out, out_shape=shapes, in_specs=[vmem] * 4, out_specs...  2.18 us

profile of v2, /device:TPU:1, one launch (start us, length us, event | category | flops | bytes accessed | tf_op | source)
XLA Modules:
  0.0 90.4 jit_solution(16758935651061626952)
XLA Ops:
  0.6 87.6 %nested_bases.1 = (f32[512,128]{1,0:T(8,128)}, f32[4,256,128]{2,1,0:T(8,128)}, f32[128,256]{1,0:T(8,128)}, f32[128,256]{1,0:T(8,128)}) custom-call(s32[15]{0:T(128)} %bitcast.12, f32[512,256]{1,0:T(8,128)} %samples.1, f32[512,256]{1,0:T(8,128)} %probes.1, f32[4096,128]{1,0:T(8,128)} %bitcast.10, f32[15,2,128,128]{3,2,1,0:T(8,128)} %bitcast.11), custom_call_target="tpu_custom_call" | custom-call | tf_op jit(solution)/shard_map/nested_bases/pallas_call | solution.py:366
  88.2 2.2 %hand_out.1 = (f32[512,128]{1,0:T(8,128)}, f32[4,256,128]{2,1,0:T(8,128)}, f32[128,256]{1,0:T(8,128)}, f32[128,256]{1,0:T(8,128)}) custom-call(f32[512,128]{1,0:T(8,128)} %get-tuple-element.12.refs_0_, f32[4,256,128]{2,1,0:T(8,128)} %get-tuple-element.13.refs_1_, f32[128,256]{1,0:T(8,128)} %get-tuple-element.14.refs_2_, f32[128,256]{1,0:T(8,128)} %get-tuple-element.15.refs_3_), custom_call_target="tpu_custom_call" | custom-call | tf_op jit(solution)/shard_map/hand_out/pallas_call | solution.py:402

commit v3 on v2

--- a/solution.py
+++ b/solution.py
@@ -100,6 +100,7 @@
     return jnp.concatenate(done, axis=0)
 
 
+NEAR_PARTS = 4
 GROUPS = 3
 
 
@@ -133,29 +134,34 @@
     def bit(i):
         return lax.rem(lax.shift_right_logical(member, jnp.int32(i)), 2)
 
+    def share(i):
+        return jnp.bitwise_xor(bit(1), bit(3)) if i == 1 and levels > 3 else bit(i)
+
     def width(t):
         return K >> t
 
     def begin(t):
         start = jnp.int32(0)
         for i in range(t):
-            start = start + bit(i) * (K >> (i + 1))
+            start = start + share(i) * (K >> (i + 1))
         return pl.multiple_of(start, BLOCK)
 
     barrier = pltpu.get_barrier_semaphore()
-    peers = [along(side << i) for i in range(levels + 1) for side in (1, -1)]
-    peers += [across(mask) for mask in range(1, leaves)]
+    peers = [along(1), along(-1)]
     for peer in peers:
         pl.semaphore_signal(barrier, inc=1, device_id=peer, device_id_type=MESH)
 
-    loads = [
-        pltpu.make_async_copy(near, near_v, local_sem.at[0]),
-        pltpu.make_async_copy(probes, probes_v, local_sem.at[1]),
-        pltpu.make_async_copy(samples, samples_v, local_sem.at[2]),
-        pltpu.make_async_copy(couplings, couplings_v, local_sem.at[3]),
-    ]
-    for load in loads:
-        load.start()
+    fetch_probes = pltpu.make_async_copy(probes, probes_v, local_sem.at[0])
+    fetch_samples = pltpu.make_async_copy(samples, samples_v, local_sem.at[1])
+    fetch_couplings = pltpu.make_async_copy(couplings, couplings_v, local_sem.at[2])
+    fetch_near = []
+    for i in range(NEAR_PARTS):
+        part = pl.ds(i * (8 * ROWS // NEAR_PARTS), 8 * ROWS // NEAR_PARTS)
+        fetch_near.append(pltpu.make_async_copy(near.at[part], near_v.at[part], local_sem.at[3 + i]))
+    fetch_probes.start()
+    for fetch in fetch_near:
+        fetch.start()
+    fetch_samples.start()
 
     def leaf_probes(half):
         return send(
@@ -180,19 +186,21 @@
             out = part if out is None else out + part
         return out
 
-    loads[0].wait()
-    loads[1].wait()
+    fetch_probes.wait()
+    for fetch in fetch_near:
+        fetch.wait()
+    fetch_couplings.start()
+    pl.semaphore_wait(barrier, len(peers))
+    leaf_probes(0).start()
     for j in range(ROWS // K):
         block = product(near_block(1, j), probes_v[...], (0, 0))
         handed[0, K * j : K * (j + 1), :] = block[:, :K]
         handed[1, K * j : K * (j + 1), :] = block[:, K:]
-    loads[2].wait()
+    leaf_handed(0).start()
+    leaf_probes(1).start()
+    leaf_handed(1).start()
+    fetch_samples.wait()
     samples_v[...] = samples_v[...] - times(0, probes_v[...])
-
-    pl.semaphore_wait(barrier, len(peers))
-    for half in range(2):
-        leaf_handed(half).start()
-        leaf_probes(half).start()
     def far_half(half):
         leaf_probes(half).wait_recv()
         upper = jnp.where(mine == total - 1, 0.0, next_probes[half])
@@ -205,14 +213,17 @@
 
     def far_copy(t, group, side):
         n = width(t)
+        device = along((2 << t) * (1 - 2 * side))
+        if t == 2 and levels > 3:
+            device["leaf"] = jnp.bitwise_xor(device["leaf"], 2)
         return send(
             sent.at[t, group, pl.ds(0, n)], far_in.at[side, t, group, pl.ds(0, n)],
-            (far_send.at[side, t, group], far_recv.at[side, t, group]), along((2 << t) * (1 - 2 * side)),
+            (far_send.at[side, t, group], far_recv.at[side, t, group]), device,
         )
 
     def pass_copy(t):
         n = width(t) // 2
-        away = pl.multiple_of((1 - bit(t)) * n, BLOCK)
+        away = pl.multiple_of((1 - share(t)) * n, BLOCK)
         return send(
             sent.at[t, :, pl.ds(away, n)], passed.at[t, :, pl.ds(0, n)],
             (pass_send.at[t], pass_recv.at[t]), across(1 << t),
@@ -222,15 +233,17 @@
         part = corrected.at[t, bit(t), pl.ds(begin(t), width(t))]
         return send(part, part, (join_send.at[t, mask], join_recv.at[t, mask]), across(mask))
 
-    def last_copy(mask):
-        part = gathered.at[:, pl.ds(begin(levels), width(levels))]
-        return send(part, part, (last_send.at[mask], last_recv.at[mask]), across(mask))
+    top = levels - 1
+
+    def last_copy(first, count, mask):
+        part = gathered.at[pl.ds(first, count), bit(top), pl.ds(begin(top), width(top))]
+        return send(part, part, (last_send.at[first, mask], last_recv.at[first, mask]), across(mask))
 
     def far_order(count):
         return sorted(range(1, count), key=lambda mask: -mask)
 
     def leaf_second():
-        loads[3].wait()
+        fetch_couplings.wait()
         far2 = far_half(1)
         tall = jnp.concatenate([far2, probes_v[:, K:], probes_v[:, :K]], axis=1)
         block = product(tall, far1[...], (0, 0))
@@ -257,6 +270,11 @@
         sent[t, 1, :n] = both[:n]
         far_copy(t, 1, 0).start()
         far_copy(t, 1, 1).start()
+        if t == top:
+            for group in (1, 2):
+                gathered[group, bit(t), pl.ds(begin(t), n)] = sent[t, group, :n]
+            for mask in far_order(leaves):
+                last_copy(1, 2, mask).start()
         own = product(gram[pl.ds(begin(t), n)], x, (1, 1))
         per = leaves >> t
         index = leaves - per + lax.shift_right_logical(member, jnp.int32(t + 1))
@@ -283,42 +301,55 @@
             join_copy(t, mask).start()
         far_copy(t, 1, 0).wait_recv()
         far_copy(t, 1, 1).wait_recv()
-        sent[t, 0, :n] = correct(both[n:], 1)
-        pass_copy(t).start()
+        second = correct(both[n:], 1)
+        if t == top:
+            gathered[0, bit(t), pl.ds(begin(t), n)] = second
+            for mask in far_order(leaves):
+                last_copy(0, 1, mask).start()
+        else:
+            sent[t, 0, :n] = second
+            pass_copy(t).start()
 
         for mask in far_order(2 << t):
             join_copy(t, mask).wait_recv()
         wide = jnp.concatenate([corrected[t, 0], corrected[t, 1]], axis=1)
         gram[...] = product(wide, wide, (1, 1))
+        if t == top:
+            return
         pass_copy(t).wait_recv()
         h = n // 2
-        keep = pl.multiple_of(bit(t) * h, BLOCK)
+        keep = pl.multiple_of(share(t) * h, BLOCK)
         kept = jnp.concatenate([sent[t, group, pl.ds(keep, h)] for group in range(GROUPS)], axis=0)
         came = jnp.concatenate([passed[t, group, :h] for group in range(GROUPS)], axis=0)
         pair = jnp.concatenate([jnp.where(even, kept, came), jnp.where(even, came, kept)], axis=1)
         block = product(pair, wide, (1, 1))
-        if t + 1 < levels:
-            for group in range(GROUPS):
-                inner[group, :h] = block[h * group : h * (group + 1)]
-        else:
-            for group in range(GROUPS):
-                gathered[group, pl.ds(begin(levels), h)] = block[h * group : h * (group + 1)]
-            for mask in far_order(leaves):
-                last_copy(mask).start()
+        for group in range(GROUPS):
+            inner[group, :h] = block[h * group : h * (group + 1)]
+
+    def last_inner(first, count):
+        for mask in far_order(leaves):
+            last_copy(first, count, mask).wait_recv()
+        wide = jnp.concatenate([corrected[top, 0], corrected[top, 1]], axis=1)
+        for group in range(first, first + count):
+            pair = jnp.concatenate([gathered[group, 0], gathered[group, 1]], axis=1)
+            inner[group] = product(pair, wide, (1, 1))
 
     def finish():
         x = inverse[...]
         level_basis(levels - 1)
         top_samples[:, :K] = product(x, gram[...], (1, 1))
-        for mask in far_order(leaves):
-            last_copy(mask).wait_recv()
-        block = product(x, jnp.concatenate([gathered[group] for group in range(GROUPS)], axis=0), (1, 1))
+        last_inner(0, 1)
+        block = product(x, jnp.concatenate([inner[group] for group in range(GROUPS)], axis=0), (1, 1))
         top_samples[:, K:] = block[:, :K]
         top_probes[:, K:] = block[:, K : 2 * K]
         top_probes[:, :K] = block[:, 2 * K :]
 
     def step(s, carry):
-        inverse[...] = inverse_factor(gram[...], {8: lambda: pl.when(s == 0)(leaf_second)})
+        def beside():
+            pl.when(s == 0)(leaf_second)
+            pl.when(s == levels)(functools.partial(last_inner, 1, 2))
+
+        inverse[...] = inverse_factor(gram[...], {8: beside})
         for t in range(levels):
             pl.when(s == t)(functools.partial(merge, t))
         pl.when(s == levels)(finish)
@@ -333,12 +364,14 @@
         for group in (2, 1):
             for side in range(2):
                 far_copy(t, group, side).wait_send()
-        pass_copy(t).wait_send()
+        if t < top:
+            pass_copy(t).wait_send()
         for mask in far_order(2 << t):
             join_copy(t, mask).wait_send()
         pltpu.make_async_copy(q_top.at[t], transfer_out.at[t], out_sem.at[t]).wait()
     for mask in far_order(leaves):
-        last_copy(mask).wait_send()
+        last_copy(1, 2, mask).wait_send()
+        last_copy(0, 1, mask).wait_send()
     pltpu.make_async_copy(q_leaf, leaf_out, out_sem.at[levels]).wait()
 
 
@@ -384,14 +417,14 @@
                 pltpu.VMEM((2, levels, GROUPS, K, K), f32),
                 pltpu.VMEM((levels, 2, K, K), f32),
                 pltpu.VMEM((levels, GROUPS, K // 2, K), f32),
-                pltpu.VMEM((GROUPS, K, K), f32),
+                pltpu.VMEM((GROUPS, 2, K, K), f32),
                 pltpu.VMEM((ROWS, K), f32),
                 pltpu.VMEM((levels, 2 * K, K), f32),
-                dma((4,)), dma((4,)), dma((4,)),
+                dma((3 + NEAR_PARTS,)), dma((4,)), dma((4,)),
                 dma((2, levels, GROUPS)), dma((2, levels, GROUPS)),
                 dma((levels,)), dma((levels,)),
                 dma((levels, leaves)), dma((levels, leaves)),
-                dma((leaves,)), dma((leaves,)),
+                dma((2, leaves)), dma((2, leaves)),
                 dma((levels + 1,)),
             ],
             compiler_params=pltpu.CompilerParams(

time: 90.5 us -> 87.2 us (0.964)
  Pallas kernels: 89.7 us -> 86.4 us
    pallas_call x1, Pallas kernels: 87.6 us -> 84.2 us  [body(): pl.pallas_call(functools.partial(kernel, leaves, subtrees), out_shape=sha...]
where the time goes in v3:
time: 87.2 us; the launch traced here: 87 us
  Pallas kernels  86.4 us (99%)
    pallas_call x1, Pallas kernels, body(): pl.pallas_call(functools.partial(kernel, leaves, subtrees), out_shape=sha...  84.2 us
    pallas_call x1, Pallas kernels, body(): pl.pallas_call(hand_out, out_shape=shapes, in_specs=[vmem] * 4, out_specs...  2.18 us

profile of v3, /device:TPU:1, one launch (start us, length us, event | category | flops | bytes accessed | tf_op | source)
XLA Modules:
  0.0 87.0 jit_solution(3395727209609809991)
XLA Ops:
  0.6 84.2 %nested_bases.1 = (f32[512,128]{1,0:T(8,128)}, f32[4,256,128]{2,1,0:T(8,128)}, f32[128,256]{1,0:T(8,128)}, f32[128,256]{1,0:T(8,128)}) custom-call(s32[15]{0:T(128)} %bitcast.12, f32[512,256]{1,0:T(8,128)} %samples.1, f32[512,256]{1,0:T(8,128)} %probes.1, f32[4096,128]{1,0:T(8,128)} %bitcast.10, f32[15,2,128,128]{3,2,1,0:T(8,128)} %bitcast.11), custom_call_target="tpu_custom_call" | custom-call | tf_op jit(solution)/shard_map/nested_bases/pallas_call | solution.py:399
  84.8 2.2 %hand_out.1 = (f32[512,128]{1,0:T(8,128)}, f32[4,256,128]{2,1,0:T(8,128)}, f32[128,256]{1,0:T(8,128)}, f32[128,256]{1,0:T(8,128)}) custom-call(f32[512,128]{1,0:T(8,128)} %get-tuple-element.12.refs_0_, f32[4,256,128]{2,1,0:T(8,128)} %get-tuple-element.13.refs_1_, f32[128,256]{1,0:T(8,128)} %get-tuple-element.14.refs_2_, f32[128,256]{1,0:T(8,128)} %get-tuple-element.15.refs_3_), custom_call_target="tpu_custom_call" | custom-call | tf_op jit(solution)/shard_map/hand_out/pallas_call | solution.py:435

commit v4 on v3

--- a/solution.py
+++ b/solution.py
@@ -209,7 +209,9 @@
         return part - jnp.where(mine == 0, 0.0, handed_in[half])
 
     far1[...] = far_half(0)
-    gram[...] = product(far1[...], far1[...], (0, 0))
+    block = product(jnp.concatenate([far1[...], probes_v[:, :K]], axis=1), far1[...], (0, 0))
+    gram[...] = block[:K]
+    inner[2] = block[K:]
 
     def far_copy(t, group, side):
         n = width(t)
@@ -221,12 +223,13 @@
             (far_send.at[side, t, group], far_recv.at[side, t, group]), device,
         )
 
-    def pass_copy(t):
+    def pass_copy(t, first, count):
         n = width(t) // 2
         away = pl.multiple_of((1 - share(t)) * n, BLOCK)
+        groups = pl.ds(first, count)
         return send(
-            sent.at[t, :, pl.ds(away, n)], passed.at[t, :, pl.ds(0, n)],
-            (pass_send.at[t], pass_recv.at[t]), across(1 << t),
+            sent.at[t, groups, pl.ds(away, n)], passed.at[t, groups, pl.ds(0, n)],
+            (pass_send.at[t, first], pass_recv.at[t, first]), across(1 << t),
         )
 
     def join_copy(t, mask):
@@ -245,10 +248,9 @@
     def leaf_second():
         fetch_couplings.wait()
         far2 = far_half(1)
-        tall = jnp.concatenate([far2, probes_v[:, K:], probes_v[:, :K]], axis=1)
-        block = product(tall, far1[...], (0, 0))
-        for group in range(GROUPS):
-            inner[group] = block[K * group : K * (group + 1)]
+        block = product(jnp.concatenate([far2, probes_v[:, K:]], axis=1), far1[...], (0, 0))
+        inner[0] = block[:K]
+        inner[1] = block[K:]
 
     def leaf_basis():
         q_leaf[...] = product(far1[...], inverse[...], (1, 1))
@@ -259,6 +261,43 @@
         for child in range(2):
             q_top[t, K * child : K * (child + 1), :] = product(corrected[t, child], x, (0, 1))
         pltpu.make_async_copy(q_top.at[t], transfer_out.at[t], out_sem.at[t]).start()
+
+    def kept_pair(t, group):
+        h = width(t) // 2
+        own = sent[t, group, pl.ds(pl.multiple_of(share(t) * h, BLOCK), h)]
+        other = passed[t, group, :h]
+        even = bit(t) == 0
+        return jnp.concatenate([jnp.where(even, own, other), jnp.where(even, other, own)], axis=1)
+
+    def children(t):
+        return jnp.concatenate([corrected[t, 0], corrected[t, 1]], axis=1)
+
+    def coupling_sides(t):
+        index = leaves - (leaves >> t) + lax.shift_right_logical(member, jnp.int32(t + 1))
+        coupling = couplings_v[slots[index], bit(t)]
+        turned = coupling.T
+        even = bit(t) == 0
+        return jnp.concatenate([jnp.where(even, coupling, turned), jnp.where(even, turned, coupling)], axis=1)
+
+    def correct(t, z, group, sides):
+        n = width(t)
+        node = lax.shift_right_logical(mine, jnp.int32(t))
+        left = jnp.where(node >= 2, far_in[0, t, group, :n], 0.0)
+        right = jnp.where(node < (total >> t) - 2, far_in[1, t, group, :n], 0.0)
+        return z - product(jnp.concatenate([left, right], axis=1), sides, (1, 1))
+
+    def second_corrected(t, sides):
+        far_copy(t, 1, 0).wait_recv()
+        far_copy(t, 1, 1).wait_recv()
+        n = width(t)
+        second = correct(t, sent[t, 0, :n], 1, sides)
+        if t == top:
+            gathered[0, bit(t), pl.ds(begin(t), n)] = second
+            for mask in far_order(leaves):
+                last_copy(0, 1, mask).start()
+        else:
+            sent[t, 0, :n] = second
+            pass_copy(t, 0, 1).start()
 
     def merge(t):
         n = width(t)
@@ -266,8 +305,17 @@
         sent[t, 2, :n] = product(inner[2, :n], x, (1, 1))
         far_copy(t, 2, 0).start()
         far_copy(t, 2, 1).start()
+        if t == 0:
+            leaf_second()
+        else:
+            pass_copy(t - 1, 0, 1).wait_recv()
+            pairs = jnp.concatenate([kept_pair(t - 1, 0), kept_pair(t - 1, 1)], axis=0)
+            block = product(pairs, children(t - 1), (1, 1))
+            inner[0, :n] = block[:n]
+            inner[1, :n] = block[n:]
         both = product(jnp.concatenate([inner[1, :n], inner[0, :n]], axis=0), x, (1, 1))
         sent[t, 1, :n] = both[:n]
+        sent[t, 0, :n] = both[n:]
         far_copy(t, 1, 0).start()
         far_copy(t, 1, 1).start()
         if t == top:
@@ -275,56 +323,33 @@
                 gathered[group, bit(t), pl.ds(begin(t), n)] = sent[t, group, :n]
             for mask in far_order(leaves):
                 last_copy(1, 2, mask).start()
+        else:
+            pass_copy(t, 1, 2).start()
         own = product(gram[pl.ds(begin(t), n)], x, (1, 1))
-        per = leaves >> t
-        index = leaves - per + lax.shift_right_logical(member, jnp.int32(t + 1))
-        coupling = couplings_v[slots[index], bit(t)]
-        turned = coupling.T
-        even = bit(t) == 0
-        sides = jnp.concatenate([jnp.where(even, coupling, turned), jnp.where(even, turned, coupling)], axis=1)
-        node = lax.shift_right_logical(mine, jnp.int32(t))
-        has_left, has_right = node >= 2, node < (total >> t) - 2
+        sides = coupling_sides(t)
         if t == 0:
             leaf_basis()
         else:
             level_basis(t - 1)
 
-        def correct(z, group):
-            left = jnp.where(has_left, far_in[0, t, group, :n], 0.0)
-            right = jnp.where(has_right, far_in[1, t, group, :n], 0.0)
-            return z - product(jnp.concatenate([left, right], axis=1), sides, (1, 1))
-
         far_copy(t, 2, 0).wait_recv()
         far_copy(t, 2, 1).wait_recv()
-        corrected[t, bit(t), pl.ds(begin(t), n)] = correct(own, 2)
+        corrected[t, bit(t), pl.ds(begin(t), n)] = correct(t, own, 2, sides)
         for mask in far_order(2 << t):
             join_copy(t, mask).start()
-        far_copy(t, 1, 0).wait_recv()
-        far_copy(t, 1, 1).wait_recv()
-        second = correct(both[n:], 1)
-        if t == top:
-            gathered[0, bit(t), pl.ds(begin(t), n)] = second
-            for mask in far_order(leaves):
-                last_copy(0, 1, mask).start()
-        else:
-            sent[t, 0, :n] = second
-            pass_copy(t).start()
+        if t > 0:
+            second_corrected(t, sides)
 
         for mask in far_order(2 << t):
             join_copy(t, mask).wait_recv()
-        wide = jnp.concatenate([corrected[t, 0], corrected[t, 1]], axis=1)
-        gram[...] = product(wide, wide, (1, 1))
+        wide = children(t)
         if t == top:
-            return
-        pass_copy(t).wait_recv()
-        h = n // 2
-        keep = pl.multiple_of(share(t) * h, BLOCK)
-        kept = jnp.concatenate([sent[t, group, pl.ds(keep, h)] for group in range(GROUPS)], axis=0)
-        came = jnp.concatenate([passed[t, group, :h] for group in range(GROUPS)], axis=0)
-        pair = jnp.concatenate([jnp.where(even, kept, came), jnp.where(even, came, kept)], axis=1)
-        block = product(pair, wide, (1, 1))
-        for group in range(GROUPS):
-            inner[group, :h] = block[h * group : h * (group + 1)]
+            gram[...] = product(wide, wide, (1, 1))
+        else:
+            pass_copy(t, 1, 2).wait_recv()
+            block = product(jnp.concatenate([wide, kept_pair(t, 2)], axis=0), wide, (1, 1))
+            gram[...] = block[:K]
+            inner[2, : n // 2] = block[K:]
 
     def last_inner(first, count):
         for mask in far_order(leaves):
@@ -346,7 +371,7 @@
 
     def step(s, carry):
         def beside():
-            pl.when(s == 0)(leaf_second)
+            pl.when(s == 1)(lambda: second_corrected(0, coupling_sides(0)))
             pl.when(s == levels)(functools.partial(last_inner, 1, 2))
 
         inverse[...] = inverse_factor(gram[...], {8: beside})
@@ -365,7 +390,8 @@
             for side in range(2):
                 far_copy(t, group, side).wait_send()
         if t < top:
-            pass_copy(t).wait_send()
+            pass_copy(t, 0, 1).wait_send()
+            pass_copy(t, 1, 2).wait_send()
         for mask in far_order(2 << t):
             join_copy(t, mask).wait_send()
         pltpu.make_async_copy(q_top.at[t], transfer_out.at[t], out_sem.at[t]).wait()
@@ -422,7 +448,7 @@
                 pltpu.VMEM((levels, 2 * K, K), f32),
                 dma((3 + NEAR_PARTS,)), dma((4,)), dma((4,)),
                 dma((2, levels, GROUPS)), dma((2, levels, GROUPS)),
-                dma((levels,)), dma((levels,)),
+                dma((levels, 2)), dma((levels, 2)),
                 dma((levels, leaves)), dma((levels, leaves)),
                 dma((2, leaves)), dma((2, leaves)),
                 dma((levels + 1,)),

time: 87.2 us -> 85.1 us (0.976)
  Pallas kernels: 86.4 us -> 84.3 us
    pallas_call x1, Pallas kernels: 84.2 us -> 82.1 us  [body(): pl.pallas_call(functools.partial(kernel, leaves, subtrees), out_shape=sha...]
where the time goes in v4:
time: 85.1 us; the launch traced here: 85 us
  Pallas kernels  84.3 us (99%)
    pallas_call x1, Pallas kernels, body(): pl.pallas_call(functools.partial(kernel, leaves, subtrees), out_shape=sha...  82.1 us
    pallas_call x1, Pallas kernels, body(): pl.pallas_call(hand_out, out_shape=shapes, in_specs=[vmem] * 4, out_specs...  2.18 us

profile of v4, /device:TPU:1, one launch (start us, length us, event | category | flops | bytes accessed | tf_op | source)
XLA Modules:
  0.0 85.0 jit_solution(12537087754563981541)
XLA Ops:
  0.6 82.1 %nested_bases.1 = (f32[512,128]{1,0:T(8,128)}, f32[4,256,128]{2,1,0:T(8,128)}, f32[128,256]{1,0:T(8,128)}, f32[128,256]{1,0:T(8,128)}) custom-call(s32[15]{0:T(128)} %bitcast.12, f32[512,256]{1,0:T(8,128)} %samples.1, f32[512,256]{1,0:T(8,128)} %probes.1, f32[4096,128]{1,0:T(8,128)} %bitcast.10, f32[15,2,128,128]{3,2,1,0:T(8,128)} %bitcast.11), custom_call_target="tpu_custom_call" | custom-call | tf_op jit(solution)/shard_map/nested_bases/pallas_call | solution.py:425
  82.8 2.2 %hand_out.1 = (f32[512,128]{1,0:T(8,128)}, f32[4,256,128]{2,1,0:T(8,128)}, f32[128,256]{1,0:T(8,128)}, f32[128,256]{1,0:T(8,128)}) custom-call(f32[512,128]{1,0:T(8,128)} %get-tuple-element.12.refs_0_, f32[4,256,128]{2,1,0:T(8,128)} %get-tuple-element.13.refs_1_, f32[128,256]{1,0:T(8,128)} %get-tuple-element.14.refs_2_, f32[128,256]{1,0:T(8,128)} %get-tuple-element.15.refs_3_), custom_call_target="tpu_custom_call" | custom-call | tf_op jit(solution)/shard_map/hand_out/pallas_call | solution.py:461

commit v5 on v4

--- a/solution.py
+++ b/solution.py
@@ -34,7 +34,7 @@
     return jnp.broadcast_to(block[:, column : column + 1], (block.shape[0], K))
 
 
-def inverse_factor(gram, interludes):
+def inverse_factor(gram):
     panels = K // BLOCK
     lane = lax.broadcasted_iota(jnp.int32, (BLOCK, K), 1)
     sub = lax.broadcasted_iota(jnp.int32, (BLOCK, K), 0)
@@ -43,8 +43,6 @@
     pivot = [spread(rows[0], i) for i in range(BLOCK)]
     done = []
     for k in range(panels):
-        if k in interludes:
-            interludes[k]()
         first, after = BLOCK * k, BLOCK * (k + 1)
         near_end = min(panels, k + 1 + REACH)
         inside = (lane >= first) & (lane < after)
@@ -246,7 +244,6 @@
         return sorted(range(1, count), key=lambda mask: -mask)
 
     def leaf_second():
-        fetch_couplings.wait()
         far2 = far_half(1)
         block = product(jnp.concatenate([far2, probes_v[:, K:]], axis=1), far1[...], (0, 0))
         inner[0] = block[:K]
@@ -306,8 +303,16 @@
         far_copy(t, 2, 0).start()
         far_copy(t, 2, 1).start()
         if t == 0:
+            fetch_couplings.wait()
+        if t == 1:
+            second_corrected(0, coupling_sides(0))
+        own = product(gram[pl.ds(begin(t), n)], x, (1, 1))
+        sides = coupling_sides(t)
+        if t == 0:
             leaf_second()
         else:
+            if t == 1:
+                level_basis(0)
             pass_copy(t - 1, 0, 1).wait_recv()
             pairs = jnp.concatenate([kept_pair(t - 1, 0), kept_pair(t - 1, 1)], axis=0)
             block = product(pairs, children(t - 1), (1, 1))
@@ -325,11 +330,9 @@
                 last_copy(1, 2, mask).start()
         else:
             pass_copy(t, 1, 2).start()
-        own = product(gram[pl.ds(begin(t), n)], x, (1, 1))
-        sides = coupling_sides(t)
         if t == 0:
             leaf_basis()
-        else:
+        elif t > 1:
             level_basis(t - 1)
 
         far_copy(t, 2, 0).wait_recv()
@@ -363,6 +366,7 @@
         x = inverse[...]
         level_basis(levels - 1)
         top_samples[:, :K] = product(x, gram[...], (1, 1))
+        last_inner(1, 2)
         last_inner(0, 1)
         block = product(x, jnp.concatenate([inner[group] for group in range(GROUPS)], axis=0), (1, 1))
         top_samples[:, K:] = block[:, :K]
@@ -370,11 +374,7 @@
         top_probes[:, :K] = block[:, 2 * K :]
 
     def step(s, carry):
-        def beside():
-            pl.when(s == 1)(lambda: second_corrected(0, coupling_sides(0)))
-            pl.when(s == levels)(functools.partial(last_inner, 1, 2))
-
-        inverse[...] = inverse_factor(gram[...], {8: beside})
+        inverse[...] = inverse_factor(gram[...])
         for t in range(levels):
             pl.when(s == t)(functools.partial(merge, t))
         pl.when(s == levels)(finish)
@@ -401,10 +401,25 @@
     pltpu.make_async_copy(q_leaf, leaf_out, out_sem.at[levels]).wait()
 
 
-def hand_out(*refs):
-    count = len(refs) // 2
-    for i in range(count):
-        refs[count + i][...] = refs[i][...]
+def hand_out(levels, *refs):
+    sources, targets, held, (in_sem, out_sem) = refs[:4], refs[4:8], refs[8:12], refs[12:]
+    pieces = [(1, t) for t in range(levels)] + [(0, None), (2, None), (3, None)]
+    pick = lambda ref, t: ref if t is None else ref.at[t]
+    reads = [
+        pltpu.make_async_copy(pick(sources[i], t), pick(held[i], t), in_sem.at[n])
+        for n, (i, t) in enumerate(pieces)
+    ]
+    writes = [
+        pltpu.make_async_copy(pick(held[i], t), pick(targets[i], t), out_sem.at[n])
+        for n, (i, t) in enumerate(pieces)
+    ]
+    for read in reads:
+        read.start()
+    for read, write in zip(reads, writes):
+        read.wait()
+        write.start()
+    for write in writes:
+        write.wait()
 
 
 def solution(mesh):
@@ -459,10 +474,11 @@
             name="nested_bases",
         )(node_slot[0], samples, probes, near, couplings[0])
         leaf_basis, transfer, top_samples, top_probes = pl.pallas_call(
-            hand_out,
+            functools.partial(hand_out, levels),
             out_shape=shapes,
-            in_specs=[vmem] * 4,
-            out_specs=(vmem,) * 4,
+            in_specs=[anywhere] * 4,
+            out_specs=(anywhere,) * 4,
+            scratch_shapes=[pltpu.VMEM(shape.shape, f32) for shape in shapes] + [dma((levels + 3,))] * 2,
             name="hand_out",
         )(*results)
         return leaf_basis, transfer[None], top_samples[None], top_probes[None]

time: 85.1 us -> 84.5 us (level)
  no operation moved by 1% of the time
where the time goes in v5:
time: 84.5 us; the launch traced here: 84.3 us
  Pallas kernels  83.7 us (99%)
    pallas_call x1, Pallas kernels, body(): pl.pallas_call(functools.partial(kernel, leaves, subtrees), out_shape=sha...  81.6 us
    pallas_call x1, Pallas kernels, body(): pl.pallas_call(functools.partial(hand_out, levels), out_shape=shapes, in_...  2.12 us

profile of v5, /device:TPU:1, one launch (start us, length us, event | category | flops | bytes accessed | tf_op | source)
XLA Modules:
  0.0 84.3 jit_solution(7845685072847057415)
XLA Ops:
  0.6 81.6 %nested_bases.1 = (f32[512,128]{1,0:T(8,128)}, f32[4,256,128]{2,1,0:T(8,128)}, f32[128,256]{1,0:T(8,128)}, f32[128,256]{1,0:T(8,128)}) custom-call(s32[15]{0:T(128)} %bitcast.12, f32[512,256]{1,0:T(8,128)} %samples.1, f32[512,256]{1,0:T(8,128)} %probes.1, f32[4096,128]{1,0:T(8,128)} %bitcast.10, f32[15,2,128,128]{3,2,1,0:T(8,128)} %bitcast.11), custom_call_target="tpu_custom_call" | custom-call | tf_op jit(solution)/shard_map/nested_bases/pallas_call | solution.py:440
  82.2 2.1 %hand_out.1 = (f32[512,128]{1,0:T(8,128)}, f32[4,256,128]{2,1,0:T(8,128)}, f32[128,256]{1,0:T(8,128)}, f32[128,256]{1,0:T(8,128)}) custom-call(f32[512,128]{1,0:T(8,128)} %get-tuple-element.12.refs_0_, f32[4,256,128]{2,1,0:T(8,128)} %get-tuple-element.13.refs_1_, f32[128,256]{1,0:T(8,128)} %get-tuple-element.14.refs_2_, f32[128,256]{1,0:T(8,128)} %get-tuple-element.15.refs_3_), custom_call_target="tpu_custom_call" | custom-call | tf_op jit(solution)/shard_map/hand_out/pallas_call | solution.py:476
